TPU v7x, 32 devices: a whole 2x2x4 slice. The times are simulated.
32 devices in a mesh: wide: 16 (over z, y, core), narrow: 2 (over x).
Axes of the slice: x: 2, y: 2, z: 4, core: 2. Of those that a mesh axis runs over, the one named last changes fastest.
Arguments:
- tensor: bfloat16 [4, 1024, 2048], P('narrow', 'wide'), may hold values from -6 to 6
- factor_a: bfloat16 [32, 1024], P(None, 'wide'), may hold values from -0.4375 to 0.4375
- factor_b: bfloat16 [32, 2048], P(None, 'wide'), may hold values from -0.3125 to 0.3125
- factor_c: bfloat16 [32, 4], P(None, 'narrow'), may hold values from -6 to 6
Outputs:
- step_a: float32 [32, 1024], P(None, 'wide')
- step_b: float32 [32, 2048], P(None, 'wide')
- step_c: float32 [32, 4], P(None, 'narrow')
All inputs are finite; a program needn't handle non-finite values.
Results may differ from a plain program's by a relative error of at most 0.0029.
Values may be sent and summed in bfloat16 or wider, within the bound.
A program may use at most 64 MiB of HBM per device.

v0:
```python
import jax
import jax.numpy as jnp
from jax import lax
from jax.sharding import PartitionSpec as P

ITERS = 2


damping = 1.0
highest = lax.Precision.HIGHEST


def matmul(left, right):
    return jnp.dot(left, right, precision=highest)


def outer_rows(left, right):
    return lax.dot_general(left, right, (((1,), (1,)), ((), ())), precision=highest)


def combine_dot(wide_part, narrow_part):
    return lax.psum(wide_part, "wide") + lax.psum(narrow_part, "narrow")


def self_inner(triple):
    return combine_dot(
        jnp.sum(triple[0] * triple[0]) + jnp.sum(triple[1] * triple[1]),
        jnp.sum(triple[2] * triple[2]),
    )


def gram_product(factors, grams, directions):
    float_a, float_b, float_c = factors
    gram_a, gram_b, gram_c = grams
    dir_a, dir_b, dir_c = directions
    local_a = outer_rows(float_a, dir_a)
    local_b = outer_rows(float_b, dir_b)
    local_c = outer_rows(float_c, dir_c)
    self_a_own = outer_rows(dir_a, dir_a)
    self_b_own = outer_rows(dir_b, dir_b)
    self_c_own = outer_rows(dir_c, dir_c)
    cross_a, cross_b, self_a, self_b = lax.psum((local_a, local_b, self_a_own, self_b_own), "wide")
    cross_c, self_c = lax.psum((local_c, self_c_own), "narrow")
    hadamard_a = gram_b * gram_c
    hadamard_b = gram_a * gram_c
    hadamard_c = gram_a * gram_b
    mixed_a = cross_b * gram_c + gram_b * cross_c
    mixed_b = cross_a * gram_c + gram_a * cross_c
    mixed_c = cross_a * gram_b + gram_a * cross_b
    image_a = matmul(hadamard_a, dir_a) + matmul(mixed_a, float_a) + damping * dir_a
    image_b = matmul(hadamard_b, dir_b) + matmul(mixed_b, float_b) + damping * dir_b
    image_c = matmul(hadamard_c, dir_c) + matmul(mixed_c, float_c) + damping * dir_c
    curvature = (
        jnp.sum(hadamard_a * self_a) + jnp.sum(mixed_a * cross_a.T) + damping * jnp.trace(self_a)
    )
    curvature = (
        curvature
        + jnp.sum(hadamard_b * self_b)
        + jnp.sum(mixed_b * cross_b.T)
        + damping * jnp.trace(self_b)
    )
    curvature = (
        curvature
        + jnp.sum(hadamard_c * self_c)
        + jnp.sum(mixed_c * cross_c.T)
        + damping * jnp.trace(self_c)
    )
    return ((image_a, image_b, image_c), curvature)


def on_device(tensor, factor_a, factor_b, factor_c):
    k_local, i_local, j_whole = tensor.shape
    rank = factor_a.shape[0]
    j_local = factor_b.shape[1]
    flattened = tensor.reshape(k_local * i_local, j_whole)
    contracted = lax.dot_general(
        lax.all_gather(factor_b, "wide", axis=1, tiled=True),
        flattened,
        (((1,), (1,)), ((), ())),
        preferred_element_type=jnp.float32,
    ).reshape(rank, k_local, i_local)
    float_a = factor_a.astype(jnp.float32)
    float_b = factor_b.astype(jnp.float32)
    float_c = factor_c.astype(jnp.float32)
    part_a = jnp.einsum("rk,rki->ri", float_c, contracted, precision=highest)
    part_c = jnp.einsum("ri,rki->rk", float_a, contracted, precision=highest)
    own_gram_a = jnp.dot(factor_a, factor_a.T, preferred_element_type=jnp.float32)
    own_gram_b = jnp.dot(factor_b, factor_b.T, preferred_element_type=jnp.float32)
    own_gram_c = jnp.dot(factor_c, factor_c.T, preferred_element_type=jnp.float32)
    mttkrp_a, gram_c = lax.psum((part_a, own_gram_c), "narrow")
    mttkrp_c, gram_a, gram_b = lax.psum((part_c, own_gram_a, own_gram_b), "wide")
    khatri = (
        (float_c[:, :, None] * float_a[:, None, :])
        .reshape(rank, k_local * i_local)
        .astype(jnp.bfloat16)
    )
    partial_b = jnp.dot(khatri, flattened, preferred_element_type=jnp.float32)
    total_b = lax.psum(partial_b, ("wide", "narrow"))
    mttkrp_b = lax.dynamic_slice_in_dim(total_b, lax.axis_index("wide") * j_local, j_local, 1)
    grad_a = matmul(gram_b * gram_c, float_a) - mttkrp_a
    grad_b = matmul(gram_a * gram_c, float_b) - mttkrp_b
    grad_c = matmul(gram_a * gram_b, float_c) - mttkrp_c
    factors = (float_a, float_b, float_c)
    grams = (gram_a, gram_b, gram_c)
    resid = (-grad_a, -grad_b, -grad_c)
    direction = resid
    steps = (jnp.zeros_like(grad_a), jnp.zeros_like(grad_b), jnp.zeros_like(grad_c))
    norm_now = self_inner(resid)
    for iteration in range(ITERS):
        image, curvature = gram_product(factors, grams, direction)
        step_size = norm_now / curvature
        steps = tuple((old + step_size * move for old, move in zip(steps, direction)))
        if iteration + 1 < ITERS:
            resid = tuple((old - step_size * move for old, move in zip(resid, image)))
            norm_next = self_inner(resid)
            momentum = norm_next / norm_now
            direction = tuple((now + momentum * old for now, old in zip(resid, direction)))
            norm_now = norm_next
    return (steps[0], steps[1], steps[2])


def solution(mesh):
    placed = (P("narrow", "wide", None), P(None, "wide"), P(None, "wide"), P(None, "narrow"))
    return jax.shard_map(
        on_device,
        mesh=mesh,
        in_specs=placed,
        out_specs=(P(None, "wide"), P(None, "wide"), P(None, "narrow")),
        check_vma=False,
    )
```

profile of v0, /device:TPU:0, one launch (start us, length us, event | category | flops | bytes accessed | tf_op | source)
XLA Modules:
  0.0 349.0 jit_solution(17142475289748499439)
XLA Ops:
  7.2 0.7 convert_element_type.12
  8.2 1.0 convolution_bitcast_fusion
  9.5 0.5 copy-done.2
  10.0 23.4 %all_gather.3 = bf16[32,2048]{1,0:T(8,128)(2,1)S(1)} all-gather(bf16[32,128]{1,0:T(8,128)(2,1)S(1)} %copy-done.2), channel_id=1, replica_groups=mesh['wide'=16,'narrow'=2] {'wide'}, dimensions={1}, use_global_device_ids=true | all-gather | bytes 139264 | tf_op jit(solution)/shard_map/all_gather | solution.py:77
  33.5 0.6 copy-done.1
  34.3 0.3 fusion.9
  34.7 57.9 %all-reduce.2 = (f32[32,32]{1,0:T(8,128)S(1)}, f32[32,32]{1,0:T(8,128)S(1)}) all-reduce(f32[32,32]{1,0:T(8,128)S(1)} %fusion.44, f32[32,32]{1,0:T(8,128)S(1)} %fusion.46), channel_id=1, replica_groups=mesh['wide'=16,'narrow'=2] {'wide'}, use_global_device_ids=true, to_apply=%region_0.0 | all-reduce | flops 2048 | bytes 16384 | tf_op jit(solution)/shard_map/psum | solution.py:91
  92.9 8.4 %all-reduce.5 = (f32[32,64]{1,0:T(8,128)S(1)}, f32[32,32]{0,1:T(8,128)S(1)}) all-reduce(f32[32,64]{1,0:T(8,128)S(1)} %bitcast.76, f32[32,32]{0,1:T(8,128)S(1)} %fusion.45), channel_id=1, replica_groups=mesh['wide'=16,'narrow'=2] {'narrow'}, use_global_device_ids=true, to_apply=%region_2.0 | all-reduce | flops 3072 | bytes 24576 | tf_op jit(solution)/shard_map/psum | solution.py:90
  101.3 0.8 multiply_reduce_fusion.9
  103.1 38.4 %all-reduce.8.cloned.1.call-done = f32[32,2048]{1,0:T(8,128)} async-done(((f32[32,2048]{1,0:T(8,128)}), f32[32,2048]{1,0:T(8,128)}) %all-reduce.8.cloned.1.call-update) | async-done | bytes 262160 | tf_op jit(solution)/shard_map/psum | solution.py:98
  141.4 1.5 multiply_reduce_fusion.8
  144.6 59.9 %all-reduce.1 = (f32[32,2]{0,1:T(2,128)S(1)}, f32[32,32]{1,0:T(8,128)S(1)}, f32[]{:T(128)}, f32[32,32]{0,1:T(8,128)S(1)}, f32[32,32]{0,1:T(8,128)S(1)}, /*index=5*/f32[32,32]{0,1:T(8,128)S(1)}) all-reduce(f32[32,2]{0,1:T(2,128)S(1)} %bitcast.78, ...), channel_id=1, replica_groups=mesh['wide'=16,'narrow'=2] {'wide'}, use_global_device_ids=true, to_apply=%region_8.0 | all-reduce | flops 4161 | bytes 33288 | tf_op jit(solution)/shard_map/psum | solution.py:91
  204.4 0.7 multiply_reduce_fusion.11
  205.8 9.5 %all-reduce.4 = (f32[32,32]{0,1:T(8,128)S(1)}, f32[]{:T(128)}, f32[32,32]{0,1:T(8,128)S(1)}) all-reduce(f32[32,32]{0,1:T(8,128)S(1)} %convolution_bitcast_fusion.5, f32[]{:T(128)} %get-tuple-element.49, f32[32,32]{0,1:T(8,128)S(1)} %fusion.37), channel_id=1, replica_groups=mesh['wide'=16,'narrow'=2] {'narrow'}, use_global_device_ids=true, to_apply=%region_14.0 | all-reduce | flops 2049 | bytes 16392 | tf_op jit(solution)/shard_map/psum | solution.py:43
  216.7 0.7 select_reduce_fusion.4
  217.4 0.7 fusion.19
  218.1 0.6 fusion.20
  224.4 0.7 multiply_reduce_fusion.4
  225.2 0.8 multiply_reduce_fusion.3
  227.4 30.0 %psum.168 = f32[]{:T(128)} all-reduce(f32[]{:T(128)S(6)} %add.179), channel_id=1, replica_groups=mesh['wide'=16,'narrow'=2] {'wide'}, use_global_device_ids=true, to_apply=%region_28.29 | all-reduce | flops 1 | bytes 8 | tf_op jit(solution)/shard_map/psum | solution.py:22
  257.4 0.7 multiply_reduce_fusion.10
  258.1 5.5 %psum.169 = f32[]{:T(128)} all-reduce(f32[]{:T(128)} %get-tuple-element.55), channel_id=1, replica_groups=mesh['wide'=16,'narrow'=2] {'narrow'}, use_global_device_ids=true, to_apply=%region_30.31 | all-reduce | flops 1 | bytes 8 | tf_op jit(solution)/shard_map/psum | solution.py:22
  266.1 57.7 %all-reduce = (f32[32,32]{0,1:T(8,128)S(1)}, f32[32,32]{1,0:T(8,128)S(1)}, f32[32,32]{0,1:T(8,128)S(1)}, f32[32,32]{0,1:T(8,128)S(1)}) all-reduce(f32[32,32]{0,1:T(8,128)S(1)} %fusion.34, f32[32,32]{1,0:T(8,128)S(1)} %convolution_bitcast_fusion.3, ...), channel_id=1, replica_groups=mesh['wide'=16,'narrow'=2] {'wide'}, use_global_device_ids=true, to_apply=%region_31.32 | all-reduce | flops 4096 | bytes 32768 | tf_op jit(solution)/shard_map/psum | solution.py:42
  323.8 0.6 select_reduce_fusion.2
  324.5 7.5 %all-reduce.3 = (f32[32,32]{0,1:T(8,128)S(1)}, f32[32,32]{0,1:T(8,128)S(1)}) all-reduce(f32[32,32]{0,1:T(8,128)S(1)} %convolution_bitcast_fusion.2, f32[32,32]{0,1:T(8,128)S(1)} %fusion.40), channel_id=1, replica_groups=mesh['wide'=16,'narrow'=2] {'narrow'}, use_global_device_ids=true, to_apply=%region_34.35 | all-reduce | flops 2048 | bytes 16384 | tf_op jit(solution)/shard_map/psum | solution.py:43
  332.0 0.7 select_reduce_fusion.1
  332.7 0.6 fusion.16
  333.4 0.7 select_reduce_fusion
  334.0 0.6 fusion.15
  340.4 0.6 multiply_add_fusion.1
  341.0 0.6 multiply_add_fusion
  341.6 0.6 multiply_add_fusion.11
  (40 shorter events, 4.5 us)
Async XLA Ops:
  7.2 1.1 copy-start
  7.2 0.8 copy-start.3
  7.2 134.2 %all-reduce.8.cloned.1.call-start = ((), (), s32[]{:S(2)}) async-start(), calls=%async_computation | async-start | bytes 524288 | tf_op jit(solution)/shard_map/psum | solution.py:98
  9.3 0.7 copy-start.2
  33.4 0.7 copy-start.1
Sparse Core Ops, SparseCore 0:
  13.5 127.8 all-reduce.7
where the time goes:
time: 350 us; the launch traced here: 349 us
  blocking collectives  260 us (74%)
  waiting for transfers between devices  38.4 us (11%)
  between operations  30.9 us (9%)
  matrix products  10.1 us (3%)
  other arithmetic  7.75 us (2%)
    psum x2, blocking collectives, on_device(): lax.psum((part_c, own_gram_a, own_gram_b), 'wide')  118 us
    psum x1, blocking collectives, gram_product(): lax.psum((local_a, local_b, self_a_own, self_b_own), 'wide')  57.7 us
    psum x1, waiting for transfers between devices, on_device(): total_b = lax.psum(partial_b, ('wide', 'narrow'))  38.4 us
    psum x2, blocking collectives, combine_dot(): return lax.psum(wide_part, 'wide') + lax.psum(narrow_part, 'narrow')  35.6 us
    all_gather x1, blocking collectives, on_device(): lax.all_gather(factor_b, 'wide', axis=1, tiled=True)  23.4 us
    psum x2, blocking collectives, gram_product(): cross_c, self_c = lax.psum((local_c, self_c_own), 'narrow')  17 us
    psum x1, blocking collectives, on_device(): mttkrp_a, gram_c = lax.psum((part_a, own_gram_c), 'narrow')  8.39 us
  transfers between devices with their start and end apart: 1, of which 1 were waited for; matrix products, arithmetic and copies ran while one was open for 1% of the time, Pallas kernels for 0%

commit v1 on v0

v1 whole, which is shorter than its diff:
```python
import functools

import jax
import jax.numpy as jnp
from jax import lax
from jax.experimental import pallas as pl
from jax.experimental.pallas import tpu as pltpu
from jax.sharding import PartitionSpec as P

MESH = pl.DeviceIdType.MESH
highest = lax.Precision.HIGHEST
damping = 1.0


def mm(left, right):
    return jnp.dot(left, right, precision=highest, preferred_element_type=jnp.float32)


def nt(left, right, precision=highest):
    return lax.dot_general(
        left, right, (((1,), (1,)), ((), ())), precision=precision, preferred_element_type=jnp.float32
    )


def total(value):
    return jnp.sum(jnp.sum(value, axis=0, keepdims=True), axis=1, keepdims=True)


def kernel(
    wide, narrow, k_local, t_hbm, a_ref, b_ref, c_ref, out_a, out_b, out_c,
    t_ref, b_all, pb_send, pb_all, q_send, q_all, w_send, w_all, m_send, m_all, s_send, s_all,
    t_sem, b_sem, pb_sem, q_sem, w_sem, m_sem, s_sem,
):
    me = lax.axis_index("wide")
    row = lax.axis_index("narrow")
    core = lax.rem(me, 2)
    chip = me // 2
    chips = wide // 2
    quad = 2 * narrow
    rank, i_local = a_ref.shape
    j_local = b_ref.shape[1]
    k_whole = narrow * k_local

    load = pltpu.make_async_copy(t_hbm, t_ref, t_sem)
    load.start()

    def wide_peer(step):
        return lax.rem(me + step, wide)

    def quad_peer(step):
        mine = row * 2 + core
        other = lax.rem(mine + step, quad)
        return other // 2, chip * 2 + lax.rem(other, 2)

    barrier = pltpu.get_barrier_semaphore()

    def greet(step, carry):
        pl.semaphore_signal(barrier, inc=1, device_id=(wide_peer(step), row), device_id_type=MESH)
        return carry

    lax.fori_loop(1, wide, greet, 0)

    def greet_row(step, carry):
        there = lax.rem(row + step, narrow)
        for side in range(2):
            pl.semaphore_signal(
                barrier, inc=1, device_id=(chip * 2 + side, there), device_id_type=MESH
            )
        return carry

    lax.fori_loop(1, narrow, greet_row, 0)
    pl.semaphore_wait(barrier, (wide - 1) + 2 * (narrow - 1))

    def send(src, dst, sems, device):
        pltpu.make_async_remote_copy(
            src_ref=src, dst_ref=dst, send_sem=sems.at[0], recv_sem=sems.at[1],
            device_id=device, device_id_type=MESH,
        ).start()

    def settle(buffer, count, sem):
        if count > 0:
            part = buffer.at[pl.ds(0, count)]
            pltpu.make_async_copy(part, part, sem).wait()

    def send_b(step, carry):
        send(b_ref, b_all.at[me], b_sem, (wide_peer(step), row))
        return carry

    lax.fori_loop(1, wide, send_b, 0)
    b_all[me] = b_ref[...]

    fa = a_ref[...].astype(jnp.float32)
    fc = c_ref[...].astype(jnp.float32)
    a_rep = jnp.concatenate([fa] * k_local, axis=1)
    c_rep = jnp.concatenate(
        [jnp.broadcast_to(fc[:, k : k + 1], (rank, i_local)) for k in range(k_local)], axis=1
    )
    khatri = (a_rep * c_rep).astype(jnp.bfloat16)
    load.wait()
    partial_b = jnp.dot(khatri, t_ref[...], preferred_element_type=jnp.float32).astype(jnp.bfloat16)
    for w in range(wide):
        pb_send[w] = partial_b[:, w * j_local : (w + 1) * j_local]

    def send_pb(step, carry):
        there = wide_peer(step)
        send(pb_send.at[there], pb_all.at[me], pb_sem, (there, row))
        return carry

    lax.fori_loop(1, wide, send_pb, 0)
    pb_all[me] = pb_send[me]
    gram_a_own = nt(fa, fa)

    settle(b_all, wide - 1, b_sem.at[1])
    factor_b = jnp.concatenate([b_all[w] for w in range(wide)], axis=1)
    contracted = nt(factor_b, t_ref[...], None)
    weighted = c_rep * contracted
    part_a = weighted[:, :i_local]
    for k in range(1, k_local):
        part_a = part_a + weighted[:, k * i_local : (k + 1) * i_local]
    pair_a = nt(a_rep, weighted)
    pair_b = nt(contracted, khatri.astype(jnp.float32))
    lane = lax.broadcasted_iota(jnp.int32, (rank, 128), 1)
    used = 3 * rank
    share = jnp.where(row == 0, 1.0, 0.0)
    small = jnp.concatenate(
        [pair_a, pair_b, gram_a_own * share, jnp.zeros((rank, 128 - used), jnp.float32)], axis=1
    )
    first = jnp.where(me == 0, 1.0, 0.0)
    product = a_rep * contracted
    for k in range(k_local):
        at = used + row * k_local + k
        column = jnp.sum(product[:, k * i_local : (k + 1) * i_local], axis=1, keepdims=True)
        small = small + jnp.where(lane == at, column, 0.0)
        small = small + jnp.where(lane == at + k_whole, fc[:, k : k + 1] * first, 0.0)
    q_send[...] = small
    q_all[row * 2 + core] = small

    def send_q(step, carry):
        there_row, there = quad_peer(step)
        send(q_send, q_all.at[row * 2 + core], q_sem, (there, there_row))
        return carry

    lax.fori_loop(1, quad, send_q, 0)

    settle(pb_all, wide - 1, pb_sem.at[1])
    part_b = jnp.sum(pb_all[...].astype(jnp.float32), axis=0)
    m_send[0] = part_b
    m_send[1, :, :i_local] = part_a
    m_all[row] = m_send[...]

    def send_m(step, carry):
        there = lax.rem(row + step, narrow)
        send(m_send, m_all.at[row], m_sem, (me, there))
        return carry

    gram_b = nt(factor_b, factor_b, None)
    settle(q_all, quad - 1, q_sem.at[1])
    small = jnp.sum(q_all[...], axis=0)
    w_send[...] = small
    w_all[chip] = small

    def send_w(step, carry):
        there = lax.rem(chip + step, chips)
        send(w_send, w_all.at[chip], w_sem, (there * 2 + core, row))
        return carry

    lax.fori_loop(1, chips, send_w, 0)
    lax.fori_loop(1, narrow, send_m, 0)
    settle(w_all, chips - 1, w_sem.at[1])
    small = jnp.sum(w_all[...], axis=0)

    pair_a = small[:, :rank]
    pair_b = small[:, rank : 2 * rank]
    gram_a = small[:, 2 * rank : used]
    mttkrp_c = small[:, used : used + k_whole]
    whole_c = small[:, used + k_whole : used + 2 * k_whole]
    fb = b_ref[...].astype(jnp.float32)

    gram_c = nt(whole_c, whole_c)
    had_a = gram_b * gram_c
    had_b = gram_a * gram_c
    had_c = gram_a * gram_b
    grad_c = mttkrp_c - mm(had_c, whole_c)
    cross_a = pair_a - mm(gram_a, had_a)
    cross_b = pair_b - mm(gram_b, had_b)
    cross_c = nt(whole_c, grad_c)
    mixed_a = cross_b * gram_c + gram_b * cross_c
    mixed_b = cross_a * gram_c + gram_a * cross_c
    mixed_c = cross_a * gram_b + gram_a * cross_b

    settle(m_all, narrow - 1, m_sem.at[1])
    summed = jnp.sum(m_all[...], axis=0)
    grad_a = summed[1][:, :i_local] - mm(had_a, fa)
    grad_b = summed[0] - mm(had_b, fb)

    had_grad_a = mm(had_a, grad_a)
    had_grad_b = mm(had_b, grad_b)
    had_grad_c = mm(had_c, grad_c)
    image_a = had_grad_a + mm(mixed_a, fa) + damping * grad_a
    image_b = had_grad_b + mm(mixed_b, fb) + damping * grad_b
    image_c = had_grad_c + mm(mixed_c, whole_c) + damping * grad_c
    sums = (
        total(grad_a * grad_a) + total(grad_b * grad_b),
        total(grad_a * had_grad_a) + total(grad_b * had_grad_b),
        total(image_a * image_a) + total(image_b * image_b),
        total(image_a * mm(had_a, image_a)) + total(image_b * mm(had_b, image_b)),
    )
    line = lax.broadcasted_iota(jnp.int32, (8, 128), 0)
    tile = jnp.zeros((8, 128), jnp.float32)
    for at, value in enumerate(sums):
        tile = jnp.where(line == at, value, tile)
    s_send[...] = tile
    s_all[me] = tile

    def send_s(step, carry):
        send(s_send, s_all.at[me], s_sem, (wide_peer(step), row))
        return carry

    lax.fori_loop(1, wide, send_s, 0)

    next_a = mm(cross_a, had_a) + damping * cross_a + nt(gram_a, mixed_a)
    next_b = mm(cross_b, had_b) + damping * cross_b + nt(gram_b, mixed_b)
    next_c = nt(whole_c, image_c)
    later_a = next_b * gram_c + gram_b * next_c
    later_b = next_a * gram_c + gram_a * next_c
    later_c = next_a * gram_b + gram_a * next_b
    known_gg = total(grad_c * grad_c)
    known_gh = total(grad_c * had_grad_c) + total(
        mixed_a * cross_a.T + mixed_b * cross_b.T + mixed_c * cross_c.T
    )
    known_qq = total(image_c * image_c)
    known_qh = total(image_c * mm(had_c, image_c)) + total(
        later_a * next_a.T + later_b * next_b.T + later_c * next_c.T
    )

    settle(s_all, wide - 1, s_sem.at[1])
    tile = jnp.sum(s_all[...], axis=0)
    norm_0 = tile[0:1, 0:1] + known_gg
    curve_0 = tile[1:2, 0:1] + known_gh + damping * norm_0
    image_2 = tile[2:3, 0:1] + known_qq
    image_3 = tile[3:4, 0:1] + known_qh + damping * image_2

    alpha_0 = norm_0 / curve_0
    norm_1 = norm_0 - 2.0 * alpha_0 * curve_0 + alpha_0 * alpha_0 * image_2
    beta = norm_1 / norm_0
    gain = 1.0 + beta
    curve_1 = gain * gain * curve_0 - 2.0 * gain * alpha_0 * image_2 + alpha_0 * alpha_0 * image_3
    alpha_1 = norm_1 / curve_1
    on_grad = alpha_0 + alpha_1 * gain
    on_image = -alpha_1 * alpha_0
    out_a[...] = on_grad * grad_a + on_image * image_a
    out_b[...] = on_grad * grad_b + on_image * image_b
    step_c = on_grad * grad_c + on_image * image_c
    lane_c = lax.broadcasted_iota(jnp.int32, (rank, k_whole), 1)
    for k in range(k_local):
        picked = jnp.where(lane_c == row * k_local + k, step_c, 0.0)
        out_c[:, k : k + 1] = jnp.sum(picked, axis=1, keepdims=True)

    settle(b_all, wide - 1, b_sem.at[0])
    settle(pb_all, wide - 1, pb_sem.at[0])
    settle(q_all, quad - 1, q_sem.at[0])
    settle(w_all, chips - 1, w_sem.at[0])
    settle(m_all, narrow - 1, m_sem.at[0])
    settle(s_all, wide - 1, s_sem.at[0])


def on_device(wide, narrow, tensor, factor_a, factor_b, factor_c):
    k_local, i_local, j_whole = tensor.shape
    rank, j_local = factor_b.shape
    flattened = tensor.reshape(k_local * i_local, j_whole)
    vmem = pl.BlockSpec(memory_space=pltpu.VMEM)
    pair = pltpu.SemaphoreType.DMA((2,))
    f32, bf16 = jnp.float32, jnp.bfloat16
    return pl.pallas_call(
        functools.partial(kernel, wide, narrow, k_local),
        out_shape=(
            jax.ShapeDtypeStruct((rank, i_local), f32),
            jax.ShapeDtypeStruct((rank, j_local), f32),
            jax.ShapeDtypeStruct((rank, k_local), f32),
        ),
        in_specs=[pl.BlockSpec(memory_space=pl.ANY), vmem, vmem, vmem],
        out_specs=(vmem, vmem, vmem),
        scratch_shapes=[
            pltpu.VMEM((k_local * i_local, j_whole), bf16),
            pltpu.VMEM((wide, rank, j_local), bf16),
            pltpu.VMEM((wide, rank, j_local), bf16),
            pltpu.VMEM((wide, rank, j_local), bf16),
            pltpu.VMEM((rank, 128), f32),
            pltpu.VMEM((2 * narrow, rank, 128), f32),
            pltpu.VMEM((rank, 128), f32),
            pltpu.VMEM((wide // 2, rank, 128), f32),
            pltpu.VMEM((2, rank, 128), f32),
            pltpu.VMEM((narrow, 2, rank, 128), f32),
            pltpu.VMEM((8, 128), f32),
            pltpu.VMEM((wide, 8, 128), f32),
            pltpu.SemaphoreType.DMA,
            pair, pair, pair, pair, pair, pair,
        ],
        compiler_params=pltpu.CompilerParams(
            collective_id=0, has_side_effects=True, vmem_limit_bytes=48 * 1024 * 1024
        ),
    )(flattened, factor_a, factor_b, factor_c)


def solution(mesh):
    placed = (P("narrow", "wide", None), P(None, "wide"), P(None, "wide"), P(None, "narrow"))
    return jax.shard_map(
        functools.partial(on_device, mesh.shape["wide"], mesh.shape["narrow"]),
        mesh=mesh,
        in_specs=placed,
        out_specs=(P(None, "wide"), P(None, "wide"), P(None, "narrow")),
        check_vma=False,
    )
```

time: 350 us -> 32 us (0.09)
  blocking collectives: 260 us -> 0 us
  waiting for transfers between devices: 38.4 us -> 0 us
  between operations: 30.9 us -> 0.66 us
  Pallas kernels: 0 us -> 26.7 us
  matrix products: 10.1 us -> 0 us
  other arithmetic: 7.75 us -> 0 us
    psum x8 -> x0, blocking collectives: 236 us -> none  [the longest x2 118 us: on_device(): lax.psum((part_c, own_gram_a, own_gram_b), 'wide')]
    psum x1 -> x0, waiting for transfers between devices: 38.4 us -> none  [on_device(): total_b = lax.psum(partial_b, ('wide', 'narrow'))]
    pallas_call x0 -> x1, Pallas kernels: none -> 26.7 us  [on_device(): pl.pallas_call(functools.partial(kernel, wide, narrow, k_local), out_shap...]
    all_gather x1 -> x0, blocking collectives: 23.4 us -> none  [on_device(): lax.all_gather(factor_b, 'wide', axis=1, tiled=True)]
    dot_general x28 -> x0, matrix products: 10.1 us -> none  [the longest x9 5.88 us: matmul(): return jnp.dot(left, right, precision=highest)]
    reduce_sum x8 -> x0, other arithmetic: 5.2 us -> none  [the longest x2 1.38 us: gram_product(): jnp.trace(self_b)]
  transfers between devices with their start and end apart: 1 -> 0, of which waited for: 1 -> 0; matrix products, arithmetic and copies ran while one was open for 1% -> 0% of each run, Pallas kernels for 0% -> 0%
where the time goes in v1:
time: 32 us; the launch traced here: 31.7 us
  Pallas kernels  26.7 us (83%)
  local copies, waits for them, and re-layouts  4.33 us (14%)
  between operations  0.66 us (2%)
    pallas_call x1, Pallas kernels, on_device(): pl.pallas_call(functools.partial(kernel, wide, narrow, k_local), out_shap...  26.7 us
    unnamed x11, local copies, waits for them, and re-layouts  3.69 us

profile of v1, /device:TPU:0, one launch (start us, length us, event | category | flops | bytes accessed | tf_op | source)
XLA Modules:
  0.0 31.7 jit_solution(15380380311267538993)
XLA Ops:
  0.6 0.0 copy-start.3
  0.6 0.0 copy-start.1
  0.7 0.6 %copy-done.3 = bf16[32,2]{0,1:T(2,128)(2,1)S(1)} copy-done((bf16[32,2]{0,1:T(2,128)(2,1)S(1)}, bf16[32,2]{0,1:T(2,128)(2,1)}, u32[]{:S(2)}) %copy-start.3) | copy-done | bytes 152
  1.3 0.1 copy.7.c_ref
  1.4 0.0 copy-done.1
  1.4 0.0 copy-start
  1.4 1.0 %copy-done = bf16[2,64,2048]{2,1,0:T(8,128)(2,1)S(1)} copy-done((bf16[2,64,2048]{2,1,0:T(8,128)(2,1)S(1)}, bf16[2,64,2048]{2,1,0:T(8,128)(2,1)}, u32[]{:S(2)}) %copy-start) | copy-done | bytes 524312
  2.4 0.0 copy-start.2
  2.4 0.7 %copy-done.2 = bf16[32,128]{1,0:T(8,128)(2,1)S(1)} copy-done((bf16[32,128]{1,0:T(8,128)(2,1)S(1)}, bf16[32,128]{1,0:T(8,128)(2,1)}, u32[]{:S(2)}) %copy-start.2) | copy-done | bytes 8216
  3.1 26.7 %shard_map.67 = (f32[32,64]{1,0:T(8,128)S(1)}, f32[32,128]{1,0:T(8,128)S(1)}, f32[32,2]{1,0:T(8,128)S(1)}) custom-call(bf16[128,2048]{1,0:T(8,128)(2,1)S(1)} %bitcast.1, bf16[32,64]{1,0:T(8,128)(2,1)S(1)} %copy-done.1, bf16[32,128]{1,0:T(8,128)(2,1)S(1)} %copy-done.2, bf16[32,2]{1,0:T(8,128)(2,1)S(1)} %copy.7.c_ref), custom_call_target="tpu_custom_call" | custom-call | tf_op jit(solution)/shard_map/pallas_call | solution.py:274
  29.9 0.6 %copy.8 = f32[32,2]{0,1:T(2,128)} copy(f32[32,2]{1,0:T(8,128)S(1)} %get-tuple-element.5) | data formatting | bytes 512 | tf_op jit(solution)/shard_map/pallas_call | solution.py:274
  30.5 0.6 %copy.11 = f32[32,64]{1,0:T(8,128)} copy(f32[32,64]{1,0:T(8,128)S(1)} %get-tuple-element.9) | data formatting | bytes 16384
  31.1 0.6 %copy.12 = f32[32,128]{1,0:T(8,128)} copy(f32[32,128]{1,0:T(8,128)S(1)} %get-tuple-element.10) | data formatting | bytes 32768
Async XLA Ops:
  0.6 0.7 %copy-start.3 = (bf16[32,2]{0,1:T(2,128)(2,1)S(1)}, bf16[32,2]{0,1:T(2,128)(2,1)}, u32[]{:S(2)}) copy-start(bf16[32,2]{0,1:T(2,128)(2,1)} %param.7) | copy-start | bytes 388
  0.6 0.7 %copy-start.1 = (bf16[32,64]{1,0:T(8,128)(2,1)S(1)}, bf16[32,64]{1,0:T(8,128)(2,1)}, u32[]{:S(2)}) copy-start(bf16[32,64]{1,0:T(8,128)(2,1)} %a_ref.1) | copy-start | bytes 12292
  1.4 1.0 %copy-start = (bf16[2,64,2048]{2,1,0:T(8,128)(2,1)S(1)}, bf16[2,64,2048]{2,1,0:T(8,128)(2,1)}, u32[]{:S(2)}) copy-start(bf16[2,64,2048]{2,1,0:T(8,128)(2,1)} %param.4) | copy-start | bytes 1572868
  2.4 0.7 %copy-start.2 = (bf16[32,128]{1,0:T(8,128)(2,1)S(1)}, bf16[32,128]{1,0:T(8,128)(2,1)}, u32[]{:S(2)}) copy-start(bf16[32,128]{1,0:T(8,128)(2,1)} %b_ref.1) | copy-start | bytes 24580

commit v2 on v1

--- a/solution.py
+++ b/solution.py
@@ -27,49 +27,61 @@
 
 
 def kernel(
-    wide, narrow, k_local, t_hbm, a_ref, b_ref, c_ref, out_a, out_b, out_c,
-    t_ref, b_all, pb_send, pb_all, q_send, q_all, w_send, w_all, m_send, m_all, s_send, s_all,
-    t_sem, b_sem, pb_sem, q_sem, w_sem, m_sem, s_sem,
+    wide, narrow, k_local, t_hbm, a_hbm, b_hbm, c_hbm, out_a, out_b, out_c,
+    t_ref, a_ref, b_ref, c_ref, b_all, pb_send, pb_all, p_send, p_all, g_all, m_send, m_all, s_all,
+    load_sem, b_sem, pb_sem, p_sem, g_sem, m_sem, s_sem,
 ):
     me = lax.axis_index("wide")
     row = lax.axis_index("narrow")
-    core = lax.rem(me, 2)
-    chip = me // 2
-    chips = wide // 2
-    quad = 2 * narrow
+    devices = wide * narrow
+    own = row * wide + me
+    owners, rows = p_send.shape[0], p_send.shape[1]
     rank, i_local = a_ref.shape
     j_local = b_ref.shape[1]
     k_whole = narrow * k_local
 
-    load = pltpu.make_async_copy(t_hbm, t_ref, t_sem)
-    load.start()
+    loads = [
+        pltpu.make_async_copy(src, dst, load_sem.at[at])
+        for at, (src, dst) in enumerate(
+            ((b_hbm, b_ref), (c_hbm, c_ref), (a_hbm, a_ref), (t_hbm, t_ref))
+        )
+    ]
+    for load in loads:
+        load.start()
 
     def wide_peer(step):
         return lax.rem(me + step, wide)
 
-    def quad_peer(step):
-        mine = row * 2 + core
-        other = lax.rem(mine + step, quad)
-        return other // 2, chip * 2 + lax.rem(other, 2)
+    def device_of(position):
+        return lax.rem(position, wide), position // wide
 
     barrier = pltpu.get_barrier_semaphore()
 
     def greet(step, carry):
-        pl.semaphore_signal(barrier, inc=1, device_id=(wide_peer(step), row), device_id_type=MESH)
-        return carry
-
-    lax.fori_loop(1, wide, greet, 0)
-
-    def greet_row(step, carry):
-        there = lax.rem(row + step, narrow)
-        for side in range(2):
-            pl.semaphore_signal(
-                barrier, inc=1, device_id=(chip * 2 + side, there), device_id_type=MESH
-            )
-        return carry
-
-    lax.fori_loop(1, narrow, greet_row, 0)
-    pl.semaphore_wait(barrier, (wide - 1) + 2 * (narrow - 1))
+        pl.semaphore_signal(
+            barrier, inc=1, device_id=device_of(lax.rem(own + step, devices)), device_id_type=MESH
+        )
+        return carry
+
+    lax.fori_loop(1, devices, greet, 0)
+    for load in loads[:3]:
+        load.wait()
+    b_all[me] = b_ref[...]
+    fa = a_ref[...].astype(jnp.float32)
+    eye = jnp.where(
+        lax.broadcasted_iota(jnp.int32, (rank, rank), 0)
+        == lax.broadcasted_iota(jnp.int32, (rank, rank), 1),
+        1.0,
+        0.0,
+    )
+    fc = nt(eye.astype(jnp.bfloat16), c_ref[...], None)
+    a_rep = jnp.concatenate([fa] * k_local, axis=1)
+    c_rep = jnp.concatenate(
+        [jnp.broadcast_to(fc[:, k : k + 1], (rank, i_local)) for k in range(k_local)], axis=1
+    )
+    khatri = (a_rep * c_rep).astype(jnp.bfloat16)
+    gram_a_own = nt(a_ref[...], a_ref[...], None)
+    pl.semaphore_wait(barrier, devices - 1)
 
     def send(src, dst, sems, device):
         pltpu.make_async_remote_copy(
@@ -87,16 +99,8 @@
         return carry
 
     lax.fori_loop(1, wide, send_b, 0)
-    b_all[me] = b_ref[...]
-
-    fa = a_ref[...].astype(jnp.float32)
-    fc = c_ref[...].astype(jnp.float32)
-    a_rep = jnp.concatenate([fa] * k_local, axis=1)
-    c_rep = jnp.concatenate(
-        [jnp.broadcast_to(fc[:, k : k + 1], (rank, i_local)) for k in range(k_local)], axis=1
-    )
-    khatri = (a_rep * c_rep).astype(jnp.bfloat16)
-    load.wait()
+
+    loads[3].wait()
     partial_b = jnp.dot(khatri, t_ref[...], preferred_element_type=jnp.float32).astype(jnp.bfloat16)
     for w in range(wide):
         pb_send[w] = partial_b[:, w * j_local : (w + 1) * j_local]
@@ -108,7 +112,6 @@
 
     lax.fori_loop(1, wide, send_pb, 0)
     pb_all[me] = pb_send[me]
-    gram_a_own = nt(fa, fa)
 
     settle(b_all, wide - 1, b_sem.at[1])
     factor_b = jnp.concatenate([b_all[w] for w in range(wide)], axis=1)
@@ -132,15 +135,47 @@
         column = jnp.sum(product[:, k * i_local : (k + 1) * i_local], axis=1, keepdims=True)
         small = small + jnp.where(lane == at, column, 0.0)
         small = small + jnp.where(lane == at + k_whole, fc[:, k : k + 1] * first, 0.0)
-    q_send[...] = small
-    q_all[row * 2 + core] = small
-
-    def send_q(step, carry):
-        there_row, there = quad_peer(step)
-        send(q_send, q_all.at[row * 2 + core], q_sem, (there, there_row))
-        return carry
-
-    lax.fori_loop(1, quad, send_q, 0)
+    p_send[...] = small.reshape(owners, rows, 128)
+
+    def send_p(step, carry):
+        owner = lax.rem(own + step, owners)
+
+        def go():
+            send(p_send.at[owner], p_all.at[own], p_sem, device_of(owner))
+
+        if owners == devices:
+            go()
+        else:
+            pl.when(owner != own)(go)
+        return carry
+
+    lax.fori_loop(1 if owners == devices else 0, owners, send_p, 0)
+    gram_b = nt(factor_b, factor_b, None)
+
+    def give():
+        p_all[own] = p_send[own]
+        settle(p_all, devices - 1, p_sem.at[1])
+        g_all[own] = jnp.sum(p_all[...], axis=0)
+
+        def send_g(step, carry):
+            there = lax.rem(own + step, devices)
+            send(g_all.at[own], g_all.at[own], g_sem, device_of(there))
+            return carry
+
+        lax.fori_loop(1, devices, send_g, 0)
+
+    def taken():
+        settle(g_all, owners - 1, g_sem.at[1])
+        settle(p_all, owners - 1, p_sem.at[0])
+
+    def taken_whole():
+        settle(g_all, owners, g_sem.at[1])
+        settle(p_all, owners, p_sem.at[0])
+
+    if owners == devices:
+        give()
+    else:
+        pl.when(own < owners)(give)
 
     settle(pb_all, wide - 1, pb_sem.at[1])
     part_b = jnp.sum(pb_all[...].astype(jnp.float32), axis=0)
@@ -153,21 +188,13 @@
         send(m_send, m_all.at[row], m_sem, (me, there))
         return carry
 
-    gram_b = nt(factor_b, factor_b, None)
-    settle(q_all, quad - 1, q_sem.at[1])
-    small = jnp.sum(q_all[...], axis=0)
-    w_send[...] = small
-    w_all[chip] = small
-
-    def send_w(step, carry):
-        there = lax.rem(chip + step, chips)
-        send(w_send, w_all.at[chip], w_sem, (there * 2 + core, row))
-        return carry
-
-    lax.fori_loop(1, chips, send_w, 0)
     lax.fori_loop(1, narrow, send_m, 0)
-    settle(w_all, chips - 1, w_sem.at[1])
-    small = jnp.sum(w_all[...], axis=0)
+    if owners == devices:
+        taken()
+    else:
+        pl.when(own < owners)(taken)
+        pl.when(own >= owners)(taken_whole)
+    small = g_all[...].reshape(rank, 128)
 
     pair_a = small[:, :rank]
     pair_b = small[:, rank : 2 * rank]
@@ -205,15 +232,14 @@
         total(image_a * image_a) + total(image_b * image_b),
         total(image_a * mm(had_a, image_a)) + total(image_b * mm(had_b, image_b)),
     )
-    line = lax.broadcasted_iota(jnp.int32, (8, 128), 0)
-    tile = jnp.zeros((8, 128), jnp.float32)
+    place = lax.broadcasted_iota(jnp.int32, (1, 128), 1)
+    tile = jnp.zeros((1, 128), jnp.float32)
     for at, value in enumerate(sums):
-        tile = jnp.where(line == at, value, tile)
-    s_send[...] = tile
+        tile = jnp.where(place == at, value, tile)
     s_all[me] = tile
 
     def send_s(step, carry):
-        send(s_send, s_all.at[me], s_sem, (wide_peer(step), row))
+        send(s_all.at[me], s_all.at[me], s_sem, (wide_peer(step), row))
         return carry
 
     lax.fori_loop(1, wide, send_s, 0)
@@ -235,10 +261,10 @@
 
     settle(s_all, wide - 1, s_sem.at[1])
     tile = jnp.sum(s_all[...], axis=0)
-    norm_0 = tile[0:1, 0:1] + known_gg
-    curve_0 = tile[1:2, 0:1] + known_gh + damping * norm_0
-    image_2 = tile[2:3, 0:1] + known_qq
-    image_3 = tile[3:4, 0:1] + known_qh + damping * image_2
+    norm_0 = tile[:, 0:1] + known_gg
+    curve_0 = tile[:, 1:2] + known_gh + damping * norm_0
+    image_2 = tile[:, 2:3] + known_qq
+    image_3 = tile[:, 3:4] + known_qh + damping * image_2
 
     alpha_0 = norm_0 / curve_0
     norm_1 = norm_0 - 2.0 * alpha_0 * curve_0 + alpha_0 * alpha_0 * image_2
@@ -251,17 +277,37 @@
     out_a[...] = on_grad * grad_a + on_image * image_a
     out_b[...] = on_grad * grad_b + on_image * image_b
     step_c = on_grad * grad_c + on_image * image_c
-    lane_c = lax.broadcasted_iota(jnp.int32, (rank, k_whole), 1)
-    for k in range(k_local):
-        picked = jnp.where(lane_c == row * k_local + k, step_c, 0.0)
-        out_c[:, k : k + 1] = jnp.sum(picked, axis=1, keepdims=True)
+    chosen = jnp.where(
+        lax.broadcasted_iota(jnp.int32, (k_local, k_whole), 1)
+        == lax.broadcasted_iota(jnp.int32, (k_local, k_whole), 0) + row * k_local,
+        1.0,
+        0.0,
+    )
+    out_c[...] = nt(chosen, step_c)
 
     settle(b_all, wide - 1, b_sem.at[0])
     settle(pb_all, wide - 1, pb_sem.at[0])
-    settle(q_all, quad - 1, q_sem.at[0])
-    settle(w_all, chips - 1, w_sem.at[0])
     settle(m_all, narrow - 1, m_sem.at[0])
     settle(s_all, wide - 1, s_sem.at[0])
+
+    def given():
+        settle(p_all, devices - 1, g_sem.at[0])
+
+    if owners == devices:
+        given()
+    else:
+        pl.when(own < owners)(given)
+
+
+def write_out(in_a, in_b, in_c, out_a, out_b, out_c, sems):
+    copies = [
+        pltpu.make_async_copy(src, dst, sems.at[at])
+        for at, (src, dst) in enumerate(((in_a, out_a), (in_b, out_b), (in_c, out_c)))
+    ]
+    for copy in copies:
+        copy.start()
+    for copy in copies:
+        copy.wait()
 
 
 def on_device(wide, narrow, tensor, factor_a, factor_b, factor_c):
@@ -269,37 +315,48 @@
     rank, j_local = factor_b.shape
     flattened = tensor.reshape(k_local * i_local, j_whole)
     vmem = pl.BlockSpec(memory_space=pltpu.VMEM)
+    anywhere = pl.BlockSpec(memory_space=pltpu.HBM)
     pair = pltpu.SemaphoreType.DMA((2,))
     f32, bf16 = jnp.float32, jnp.bfloat16
-    return pl.pallas_call(
+    owners = min(rank, wide * narrow)
+    rows = rank // owners
+    shapes = (
+        jax.ShapeDtypeStruct((rank, i_local), f32),
+        jax.ShapeDtypeStruct((rank, j_local), f32),
+        jax.ShapeDtypeStruct((k_local, rank), f32),
+    )
+    steps = pl.pallas_call(
         functools.partial(kernel, wide, narrow, k_local),
-        out_shape=(
-            jax.ShapeDtypeStruct((rank, i_local), f32),
-            jax.ShapeDtypeStruct((rank, j_local), f32),
-            jax.ShapeDtypeStruct((rank, k_local), f32),
-        ),
-        in_specs=[pl.BlockSpec(memory_space=pl.ANY), vmem, vmem, vmem],
+        out_shape=shapes,
+        in_specs=[anywhere] * 4,
         out_specs=(vmem, vmem, vmem),
         scratch_shapes=[
             pltpu.VMEM((k_local * i_local, j_whole), bf16),
+            pltpu.VMEM((rank, i_local), bf16),
+            pltpu.VMEM((rank, j_local), bf16),
+            pltpu.VMEM((k_local, rank), bf16),
             pltpu.VMEM((wide, rank, j_local), bf16),
             pltpu.VMEM((wide, rank, j_local), bf16),
             pltpu.VMEM((wide, rank, j_local), bf16),
-            pltpu.VMEM((rank, 128), f32),
-            pltpu.VMEM((2 * narrow, rank, 128), f32),
-            pltpu.VMEM((rank, 128), f32),
-            pltpu.VMEM((wide // 2, rank, 128), f32),
+            pltpu.VMEM((owners, rows, 128), f32),
+            pltpu.VMEM((wide * narrow, rows, 128), f32),
+            pltpu.VMEM((owners, rows, 128), f32),
             pltpu.VMEM((2, rank, 128), f32),
             pltpu.VMEM((narrow, 2, rank, 128), f32),
-            pltpu.VMEM((8, 128), f32),
-            pltpu.VMEM((wide, 8, 128), f32),
-            pltpu.SemaphoreType.DMA,
+            pltpu.VMEM((wide, 1, 128), f32),
+            pltpu.SemaphoreType.DMA((4,)),
             pair, pair, pair, pair, pair, pair,
         ],
-        compiler_params=pltpu.CompilerParams(
-            collective_id=0, has_side_effects=True, vmem_limit_bytes=48 * 1024 * 1024
-        ),
-    )(flattened, factor_a, factor_b, factor_c)
+        compiler_params=pltpu.CompilerParams(collective_id=0, has_side_effects=True),
+    )(flattened, factor_a, factor_b, factor_c.T)
+    step_a, step_b, step_c = pl.pallas_call(
+        write_out,
+        out_shape=shapes,
+        in_specs=[pl.BlockSpec(memory_space=pl.ANY)] * 3,
+        out_specs=(anywhere,) * 3,
+        scratch_shapes=[pltpu.SemaphoreType.DMA((3,))],
+    )(*steps)
+    return step_a, step_b, step_c.T
 
 
 def solution(mesh):

time: 32 us -> 31.8 us (level)
  local copies, waits for them, and re-layouts: 4.33 us -> 0 us
  Pallas kernels: 26.7 us -> 31 us
    unnamed x11 -> x0, local copies, waits for them, and re-layouts: 3.69 us -> none
    pallas_call x0 -> x1, Pallas kernels: none -> 2.15 us  [on_device(): pl.pallas_call(write_out, out_shape=shapes, in_specs=[pl.BlockSpec(memory...]
    pallas_call x1, Pallas kernels: 26.7 us -> 28.8 us  [on_device(): pl.pallas_call(functools.partial(kernel, wide, narrow, k_local), out_shap...]
    pallas_call x1 -> x0, local copies, waits for them, and re-layouts: 0.64 us -> none  [on_device(): pl.pallas_call(functools.partial(kernel, wide, narrow, k_local), out_shap...]
where the time goes in v2:
time: 31.8 us; the launch traced here: 31.6 us
  Pallas kernels  31 us (97%)
  between operations  0.64 us (2%)
    pallas_call x1, Pallas kernels, on_device(): pl.pallas_call(functools.partial(kernel, wide, narrow, k_local), out_shap...  28.8 us
    pallas_call x1, Pallas kernels, on_device(): pl.pallas_call(write_out, out_shape=shapes, in_specs=[pl.BlockSpec(memory...  2.15 us

profile of v2, /device:TPU:0, one launch (start us, length us, event | category | flops | bytes accessed | tf_op | source)
XLA Modules:
  0.0 31.6 jit_solution(15998219661863282469)
XLA Ops:
  0.6 28.8 %shard_map.67 = (f32[32,64]{1,0:T(8,128)}, f32[32,128]{1,0:T(8,128)}, f32[2,32]{1,0:T(2,128)}) custom-call(bf16[128,2048]{1,0:T(8,128)(2,1)} %bitcast.3, bf16[32,64]{1,0:T(8,128)(2,1)} %a_hbm.1, bf16[32,128]{1,0:T(8,128)(2,1)} %b_hbm.1, bf16[2,32]{1,0:T(2,128)(2,1)} %bitcast.4), custom_call_target="tpu_custom_call" | custom-call | tf_op jit(solution)/shard_map/pallas_call | solution.py:328
  29.5 2.2 %shard_map.68 = (f32[32,64]{1,0:T(8,128)}, f32[32,128]{1,0:T(8,128)}, f32[2,32]{1,0:T(2,128)}) custom-call(f32[32,64]{1,0:T(8,128)} %get-tuple-element.9.in_a, f32[32,128]{1,0:T(8,128)} %get-tuple-element.10.in_b, f32[2,32]{1,0:T(2,128)} %get-tuple-element.11.in_c), custom_call_target="tpu_custom_call" | custom-call | tf_op jit(solution)/shard_map/pallas_call | solution.py:352

commit v3 on v2

--- a/solution.py
+++ b/solution.py
@@ -26,10 +26,23 @@
     return jnp.sum(jnp.sum(value, axis=0, keepdims=True), axis=1, keepdims=True)
 
 
+def spread(first, last, body):
+    if last - first <= 32:
+        for step in range(first, last):
+            body(step)
+        return
+
+    def turn(step, carry):
+        body(step)
+        return carry
+
+    lax.fori_loop(first, last, turn, 0)
+
+
 def kernel(
     wide, narrow, k_local, t_hbm, a_hbm, b_hbm, c_hbm, out_a, out_b, out_c,
-    t_ref, a_ref, b_ref, c_ref, b_all, pb_send, pb_all, p_send, p_all, g_all, m_send, m_all, s_all,
-    load_sem, b_sem, pb_sem, p_sem, g_sem, m_sem, s_sem,
+    t_ref, a_ref, b_ref, c_ref, a_all, c_all, b_all, pb_send, pb_all, p_send, p_all, g_all, m_send, m_all, s_all,
+    load_sem, a_sem, c_sem, b_sem, pb_sem, p_sem, g_sem, m_sem, s_sem,
 ):
     me = lax.axis_index("wide")
     row = lax.axis_index("narrow")
@@ -57,16 +70,17 @@
 
     barrier = pltpu.get_barrier_semaphore()
 
-    def greet(step, carry):
+    def greet(step):
         pl.semaphore_signal(
             barrier, inc=1, device_id=device_of(lax.rem(own + step, devices)), device_id_type=MESH
         )
-        return carry
-
-    lax.fori_loop(1, devices, greet, 0)
+
+    spread(1, devices, greet)
     for load in loads[:3]:
         load.wait()
     b_all[me] = b_ref[...]
+    a_all[me] = a_ref[...]
+    c_all[row] = c_ref[...]
     fa = a_ref[...].astype(jnp.float32)
     eye = jnp.where(
         lax.broadcasted_iota(jnp.int32, (rank, rank), 0)
@@ -80,7 +94,9 @@
         [jnp.broadcast_to(fc[:, k : k + 1], (rank, i_local)) for k in range(k_local)], axis=1
     )
     khatri = (a_rep * c_rep).astype(jnp.bfloat16)
-    gram_a_own = nt(a_ref[...], a_ref[...], None)
+    lane_k = lax.broadcasted_iota(jnp.int32, (rank, k_local * i_local), 0)
+    from_k = lax.broadcasted_iota(jnp.int32, (rank, k_local * i_local), 1) // i_local
+    gather_k = jnp.where(lane_k == from_k + row * k_local, 1.0, 0.0)
     pl.semaphore_wait(barrier, devices - 1)
 
     def send(src, dst, sems, device):
@@ -94,23 +110,32 @@
             part = buffer.at[pl.ds(0, count)]
             pltpu.make_async_copy(part, part, sem).wait()
 
-    def send_b(step, carry):
+    def send_b(step):
         send(b_ref, b_all.at[me], b_sem, (wide_peer(step), row))
-        return carry
-
-    lax.fori_loop(1, wide, send_b, 0)
+
+    spread(1, wide, send_b)
+
+    def send_c(step):
+        there = lax.rem(row + step, narrow)
+        send(c_ref, c_all.at[row], c_sem, (me, there))
+
+    spread(1, narrow, send_c)
+
+    def send_a(step):
+        send(a_ref, a_all.at[me], a_sem, (wide_peer(step), row))
+
+    spread(1, wide, send_a)
 
     loads[3].wait()
     partial_b = jnp.dot(khatri, t_ref[...], preferred_element_type=jnp.float32).astype(jnp.bfloat16)
     for w in range(wide):
         pb_send[w] = partial_b[:, w * j_local : (w + 1) * j_local]
 
-    def send_pb(step, carry):
+    def send_pb(step):
         there = wide_peer(step)
         send(pb_send.at[there], pb_all.at[me], pb_sem, (there, row))
-        return carry
-
-    lax.fori_loop(1, wide, send_pb, 0)
+
+    spread(1, wide, send_pb)
     pb_all[me] = pb_send[me]
 
     settle(b_all, wide - 1, b_sem.at[1])
@@ -122,22 +147,13 @@
         part_a = part_a + weighted[:, k * i_local : (k + 1) * i_local]
     pair_a = nt(a_rep, weighted)
     pair_b = nt(contracted, khatri.astype(jnp.float32))
-    lane = lax.broadcasted_iota(jnp.int32, (rank, 128), 1)
-    used = 3 * rank
-    share = jnp.where(row == 0, 1.0, 0.0)
-    small = jnp.concatenate(
-        [pair_a, pair_b, gram_a_own * share, jnp.zeros((rank, 128 - used), jnp.float32)], axis=1
-    )
-    first = jnp.where(me == 0, 1.0, 0.0)
     product = a_rep * contracted
-    for k in range(k_local):
-        at = used + row * k_local + k
-        column = jnp.sum(product[:, k * i_local : (k + 1) * i_local], axis=1, keepdims=True)
-        small = small + jnp.where(lane == at, column, 0.0)
-        small = small + jnp.where(lane == at + k_whole, fc[:, k : k + 1] * first, 0.0)
+    pair_c = nt(c_rep, product)
+    column_c = nt(product, gather_k)
+    small = jnp.concatenate([pair_a, pair_b, pair_c, column_c], axis=1)
     p_send[...] = small.reshape(owners, rows, 128)
 
-    def send_p(step, carry):
+    def send_p(step):
         owner = lax.rem(own + step, owners)
 
         def go():
@@ -147,22 +163,27 @@
             go()
         else:
             pl.when(owner != own)(go)
-        return carry
-
-    lax.fori_loop(1 if owners == devices else 0, owners, send_p, 0)
-    gram_b = nt(factor_b, factor_b, None)
+
+    spread(1 if owners == devices else 0, owners, send_p)
+    settle(a_all, wide - 1, a_sem.at[1])
+    settle(c_all, narrow - 1, c_sem.at[1])
+    gram_a = nt(a_all[0], a_all[0], None)
+    for w in range(1, wide):
+        gram_a = gram_a + nt(a_all[w], a_all[w], None)
+    whole_c = jnp.concatenate(
+        [nt(eye.astype(jnp.bfloat16), c_all[n], None) for n in range(narrow)], axis=1
+    )
 
     def give():
         p_all[own] = p_send[own]
         settle(p_all, devices - 1, p_sem.at[1])
         g_all[own] = jnp.sum(p_all[...], axis=0)
 
-        def send_g(step, carry):
+        def send_g(step):
             there = lax.rem(own + step, devices)
             send(g_all.at[own], g_all.at[own], g_sem, device_of(there))
-            return carry
-
-        lax.fori_loop(1, devices, send_g, 0)
+
+        spread(1, devices, send_g)
 
     def taken():
         settle(g_all, owners - 1, g_sem.at[1])
@@ -183,42 +204,37 @@
     m_send[1, :, :i_local] = part_a
     m_all[row] = m_send[...]
 
-    def send_m(step, carry):
+    def send_m(step):
         there = lax.rem(row + step, narrow)
         send(m_send, m_all.at[row], m_sem, (me, there))
-        return carry
-
-    lax.fori_loop(1, narrow, send_m, 0)
+
+    spread(1, narrow, send_m)
+    gram_b = nt(factor_b, factor_b, None)
+    gram_c = nt(whole_c, whole_c)
+    had_a = gram_b * gram_c
+    had_b = gram_a * gram_c
+    had_c = gram_a * gram_b
+    fb = b_ref[...].astype(jnp.float32)
+    model_a, model_b, model_c = mm(had_a, fa), mm(had_b, fb), mm(had_c, whole_c)
+    inner_a, inner_b, inner_c = mm(gram_a, had_a), mm(gram_b, had_b), mm(gram_c, had_c)
+    settle(m_all, narrow - 1, m_sem.at[1])
+    summed = jnp.sum(m_all[...], axis=0)
+    grad_a = summed[1][:, :i_local] - model_a
+    grad_b = summed[0] - model_b
+
     if owners == devices:
         taken()
     else:
         pl.when(own < owners)(taken)
         pl.when(own >= owners)(taken_whole)
     small = g_all[...].reshape(rank, 128)
-
-    pair_a = small[:, :rank]
-    pair_b = small[:, rank : 2 * rank]
-    gram_a = small[:, 2 * rank : used]
-    mttkrp_c = small[:, used : used + k_whole]
-    whole_c = small[:, used + k_whole : used + 2 * k_whole]
-    fb = b_ref[...].astype(jnp.float32)
-
-    gram_c = nt(whole_c, whole_c)
-    had_a = gram_b * gram_c
-    had_b = gram_a * gram_c
-    had_c = gram_a * gram_b
-    grad_c = mttkrp_c - mm(had_c, whole_c)
-    cross_a = pair_a - mm(gram_a, had_a)
-    cross_b = pair_b - mm(gram_b, had_b)
-    cross_c = nt(whole_c, grad_c)
+    cross_a = small[:, :rank] - inner_a
+    cross_b = small[:, rank : 2 * rank] - inner_b
+    cross_c = small[:, 2 * rank : 3 * rank] - inner_c
+    grad_c = small[:, 3 * rank : 3 * rank + k_whole] - model_c
     mixed_a = cross_b * gram_c + gram_b * cross_c
     mixed_b = cross_a * gram_c + gram_a * cross_c
     mixed_c = cross_a * gram_b + gram_a * cross_b
-
-    settle(m_all, narrow - 1, m_sem.at[1])
-    summed = jnp.sum(m_all[...], axis=0)
-    grad_a = summed[1][:, :i_local] - mm(had_a, fa)
-    grad_b = summed[0] - mm(had_b, fb)
 
     had_grad_a = mm(had_a, grad_a)
     had_grad_b = mm(had_b, grad_b)
@@ -238,11 +254,10 @@
         tile = jnp.where(place == at, value, tile)
     s_all[me] = tile
 
-    def send_s(step, carry):
+    def send_s(step):
         send(s_all.at[me], s_all.at[me], s_sem, (wide_peer(step), row))
-        return carry
-
-    lax.fori_loop(1, wide, send_s, 0)
+
+    spread(1, wide, send_s)
 
     next_a = mm(cross_a, had_a) + damping * cross_a + nt(gram_a, mixed_a)
     next_b = mm(cross_b, had_b) + damping * cross_b + nt(gram_b, mixed_b)
@@ -285,6 +300,8 @@
     )
     out_c[...] = nt(chosen, step_c)
 
+    settle(a_all, wide - 1, a_sem.at[0])
+    settle(c_all, narrow - 1, c_sem.at[0])
     settle(b_all, wide - 1, b_sem.at[0])
     settle(pb_all, wide - 1, pb_sem.at[0])
     settle(m_all, narrow - 1, m_sem.at[0])
@@ -297,17 +314,6 @@
         given()
     else:
         pl.when(own < owners)(given)
-
-
-def write_out(in_a, in_b, in_c, out_a, out_b, out_c, sems):
-    copies = [
-        pltpu.make_async_copy(src, dst, sems.at[at])
-        for at, (src, dst) in enumerate(((in_a, out_a), (in_b, out_b), (in_c, out_c)))
-    ]
-    for copy in copies:
-        copy.start()
-    for copy in copies:
-        copy.wait()
 
 
 def on_device(wide, narrow, tensor, factor_a, factor_b, factor_c):
@@ -325,7 +331,7 @@
         jax.ShapeDtypeStruct((rank, j_local), f32),
         jax.ShapeDtypeStruct((k_local, rank), f32),
     )
-    steps = pl.pallas_call(
+    step_a, step_b, step_c = pl.pallas_call(
         functools.partial(kernel, wide, narrow, k_local),
         out_shape=shapes,
         in_specs=[anywhere] * 4,
@@ -335,6 +341,8 @@
             pltpu.VMEM((rank, i_local), bf16),
             pltpu.VMEM((rank, j_local), bf16),
             pltpu.VMEM((k_local, rank), bf16),
+            pltpu.VMEM((wide, rank, i_local), bf16),
+            pltpu.VMEM((narrow, k_local, rank), bf16),
             pltpu.VMEM((wide, rank, j_local), bf16),
             pltpu.VMEM((wide, rank, j_local), bf16),
             pltpu.VMEM((wide, rank, j_local), bf16),
@@ -345,17 +353,10 @@
             pltpu.VMEM((narrow, 2, rank, 128), f32),
             pltpu.VMEM((wide, 1, 128), f32),
             pltpu.SemaphoreType.DMA((4,)),
-            pair, pair, pair, pair, pair, pair,
+            pair, pair, pair, pair, pair, pair, pair, pair,
         ],
         compiler_params=pltpu.CompilerParams(collective_id=0, has_side_effects=True),
     )(flattened, factor_a, factor_b, factor_c.T)
-    step_a, step_b, step_c = pl.pallas_call(
-        write_out,
-        out_shape=shapes,
-        in_specs=[pl.BlockSpec(memory_space=pl.ANY)] * 3,
-        out_specs=(anywhere,) * 3,
-        scratch_shapes=[pltpu.SemaphoreType.DMA((3,))],
-    )(*steps)
     return step_a, step_b, step_c.T
 
 

time: 31.8 us -> 31.6 us (level)
  Pallas kernels: 31 us -> 28 us
  local copies, waits for them, and re-layouts: 0 us -> 2.53 us
    unnamed x0 -> x7, local copies, waits for them, and re-layouts: none -> 2.53 us
    pallas_call x1 -> x0, Pallas kernels: 2.15 us -> none  [on_device(): pl.pallas_call(write_out, out_shape=shapes, in_specs=[pl.BlockSpec(memory...]
    pallas_call x1, Pallas kernels: 28.8 us -> 28 us  [on_device(): pl.pallas_call(functools.partial(kernel, wide, narrow, k_local), out_shap...]
where the time goes in v3:
time: 31.6 us; the launch traced here: 31.2 us
  Pallas kernels  28 us (89%)
  local copies, waits for them, and re-layouts  2.53 us (8%)
  between operations  0.65 us (2%)
    pallas_call x1, Pallas kernels, on_device(): pl.pallas_call(functools.partial(kernel, wide, narrow, k_local), out_shap...  28 us
    unnamed x7, local copies, waits for them, and re-layouts  2.53 us

profile of v3, /device:TPU:0, one launch (start us, length us, event | category | flops | bytes accessed | tf_op | source)
XLA Modules:
  0.0 31.2 jit_solution(15812314935854770293)
XLA Ops:
  0.6 28.0 %shard_map.67 = (f32[32,64]{1,0:T(8,128)}, f32[32,128]{1,0:T(8,128)}, f32[2,32]{1,0:T(2,128)}) custom-call(bf16[128,2048]{1,0:T(8,128)(2,1)} %bitcast.3, bf16[32,64]{1,0:T(8,128)(2,1)} %a_hbm.1, bf16[32,128]{1,0:T(8,128)(2,1)} %b_hbm.1, bf16[2,32]{1,0:T(2,128)(2,1)} %bitcast.5), custom_call_target="tpu_custom_call" | custom-call | tf_op jit(solution)/shard_map/pallas_call | solution.py:334
  28.7 0.0 copy-start
  28.7 1.3 %copy.10 = f32[32,64]{1,0:T(8,128)} copy(f32[32,64]{1,0:T(8,128)} %get-tuple-element.12) | data formatting | bytes 16384
  30.0 0.0 copy-done
  30.0 0.0 copy-start.1
  30.0 0.6 %copy.11 = f32[32,128]{1,0:T(8,128)} copy(f32[32,128]{1,0:T(8,128)S(1)} %copy-done) | data formatting | bytes 32768
  30.6 0.0 copy-done.1
  30.7 0.6 %copy.12 = f32[32,2]{0,1:T(2,128)} copy(f32[32,2]{0,1:T(2,128)S(1)} %bitcast.4) | data formatting | bytes 512
Async XLA Ops:
  28.7 1.3 %copy-start = (f32[32,128]{1,0:T(8,128)S(1)}, f32[32,128]{1,0:T(8,128)}, u32[]{:S(2)}) copy-start(f32[32,128]{1,0:T(8,128)} %get-tuple-element.13) | copy-start | bytes 49156
  30.0 0.6 %copy-start.1 = (f32[2,32]{1,0:T(2,128)S(1)}, f32[2,32]{1,0:T(2,128)}, u32[]{:S(2)}) copy-start(f32[2,32]{1,0:T(2,128)} %get-tuple-element.8) | copy-start | bytes 772

commit v4 on v3

v4 whole, which is shorter than its diff:
```python
import functools

import jax
import jax.numpy as jnp
from jax import lax
from jax.experimental import pallas as pl
from jax.experimental.pallas import tpu as pltpu
from jax.sharding import PartitionSpec as P

MESH = pl.DeviceIdType.MESH
highest = lax.Precision.HIGHEST
damping = 1.0


def mm(left, right):
    return jnp.dot(left, right, precision=highest, preferred_element_type=jnp.float32)


def nt(left, right, precision=highest):
    return lax.dot_general(
        left, right, (((1,), (1,)), ((), ())), precision=precision, preferred_element_type=jnp.float32
    )


def total(value):
    return jnp.sum(jnp.sum(value, axis=0, keepdims=True), axis=1, keepdims=True)


def spread(first, last, body):
    if last - first <= 32:
        for step in range(first, last):
            body(step)
        return

    def turn(step, carry):
        body(step)
        return carry

    lax.fori_loop(first, last, turn, 0)


def kernel(
    wide, narrow, k_local, t_hbm, a_hbm, b_hbm, c_hbm, out_a, out_b, out_c,
    t_ref, a_ref, b_ref, c_ref, c_all, b_all, pb_send, pb_half, pb_all, p_send, p_all, w_all, g_all,
    m_send, m_all, s_all,
    load_sem, c_sem, b_sem, relay_sem, half_sem, pb_sem, p_sem, w_sem, g_sem, m_sem, s_sem,
):
    me = lax.axis_index("wide")
    row = lax.axis_index("narrow")
    core = lax.rem(me, 2)
    chip = me // 2
    chips = wide // 2
    quad = 2 * narrow
    mine = row * 2 + core
    partner = (chip * 2 + 1 - core, row)
    rank, i_local = a_ref.shape
    j_local = b_ref.shape[1]
    k_whole = narrow * k_local

    loads = [
        pltpu.make_async_copy(src, dst, load_sem.at[at])
        for at, (src, dst) in enumerate(
            ((b_hbm, b_ref), (c_hbm, c_ref), (a_hbm, a_ref), (t_hbm, t_ref))
        )
    ]
    for load in loads:
        load.start()

    def wide_peer(step):
        return lax.rem(me + step, wide)

    def chip_peer(step):
        return lax.rem(chip + step, chips)

    def quad_peer(step):
        other = lax.rem(mine + step, quad)
        return other, (chip * 2 + lax.rem(other, 2), other // 2)

    barrier = pltpu.get_barrier_semaphore()

    def greet(step):
        pl.semaphore_signal(barrier, inc=1, device_id=(wide_peer(step), row), device_id_type=MESH)

    def greet_row(step):
        there = lax.rem(row + step, narrow)
        for side in range(2):
            pl.semaphore_signal(
                barrier, inc=1, device_id=(chip * 2 + side, there), device_id_type=MESH
            )

    spread(1, wide, greet)
    spread(1, narrow, greet_row)
    for load in loads[:3]:
        load.wait()
    b_all[core, chip] = b_ref[...]
    c_all[row] = c_ref[...]
    fa = a_ref[...].astype(jnp.float32)
    eye = jnp.where(
        lax.broadcasted_iota(jnp.int32, (rank, rank), 0)
        == lax.broadcasted_iota(jnp.int32, (rank, rank), 1),
        1.0,
        0.0,
    )
    fc = nt(eye.astype(jnp.bfloat16), c_ref[...], None)
    a_rep = jnp.concatenate([fa] * k_local, axis=1)
    c_rep = jnp.concatenate(
        [jnp.broadcast_to(fc[:, k : k + 1], (rank, i_local)) for k in range(k_local)], axis=1
    )
    khatri = (a_rep * c_rep).astype(jnp.bfloat16)
    lane_k = lax.broadcasted_iota(jnp.int32, (rank, k_local * i_local), 0)
    from_k = lax.broadcasted_iota(jnp.int32, (rank, k_local * i_local), 1) // i_local
    gather_k = jnp.where(lane_k == from_k + row * k_local, 1.0, 0.0)
    gram_a_own = nt(a_ref[...], a_ref[...], None) * jnp.where(row == 0, 1.0, 0.0)
    pl.semaphore_wait(barrier, (wide - 1) + 2 * (narrow - 1))

    def send(src, dst, sems, device):
        pltpu.make_async_remote_copy(
            src_ref=src, dst_ref=dst, send_sem=sems.at[0], recv_sem=sems.at[1],
            device_id=device, device_id_type=MESH,
        ).start()

    def settle(buffer, count, sem):
        if count > 0:
            part = buffer.at[pl.ds(0, count)]
            pltpu.make_async_copy(part, part, sem).wait()

    def send_b(step):
        send(b_ref, b_all.at[core, chip], b_sem, (chip_peer(step) * 2 + core, row))

    spread(1, chips, send_b)

    def send_c(step):
        there = lax.rem(row + step, narrow)
        send(c_ref, c_all.at[row], c_sem, (me, there))

    spread(1, narrow, send_c)

    loads[3].wait()
    partial_b = jnp.dot(khatri, t_ref[...], preferred_element_type=jnp.float32)
    for w in range(wide):
        pb_send[w % 2, w // 2] = partial_b[:, w * j_local : (w + 1) * j_local]
    send(pb_send.at[1 - core], pb_half, half_sem, partner)

    def contract(side):
        blocks = jnp.concatenate([b_all[side, at] for at in range(chips)], axis=1)
        columns = [
            t_ref[:, pl.ds(pl.multiple_of((at * 2 + side) * j_local, j_local), j_local)]
            for at in range(chips)
        ]
        return nt(blocks, jnp.concatenate(columns, axis=1), None)

    settle(b_all.at[core], chips - 1, b_sem.at[1])
    send(b_all.at[core], b_all.at[core], relay_sem, partner)
    contracted = contract(core)
    settle(pb_half, chips, half_sem.at[1])
    for at in range(chips):
        pb_half[at] = pb_half[at] + pb_send[core, at]

    def send_pb(step):
        there = chip_peer(step)
        send(pb_half.at[there], pb_all.at[chip], pb_sem, (there * 2 + core, row))

    spread(1, chips, send_pb)
    pb_all[chip] = pb_half[chip]
    settle(b_all.at[1 - core], chips, relay_sem.at[1])
    contracted = contracted + contract(1 - core)
    weighted = c_rep * contracted
    part_a = weighted[:, :i_local]
    for k in range(1, k_local):
        part_a = part_a + weighted[:, k * i_local : (k + 1) * i_local]
    pair_a = nt(a_rep, weighted)
    pair_b = nt(contracted, khatri.astype(jnp.float32))
    product = a_rep * contracted
    column_c = nt(product, gather_k)
    small = jnp.concatenate([pair_a, pair_b, gram_a_own, column_c], axis=1)
    p_send[...] = small.reshape(p_send.shape)

    def send_p(step):
        other, there = quad_peer(step)
        send(p_send.at[other], p_all.at[mine], p_sem, there)

    spread(1, quad, send_p)
    p_all[mine] = p_send[mine]
    settle(c_all, narrow - 1, c_sem.at[1])
    whole_c = jnp.concatenate(
        [nt(eye.astype(jnp.bfloat16), c_all[n], None) for n in range(narrow)], axis=1
    )
    settle(p_all, quad - 1, p_sem.at[1])
    w_all[chip] = jnp.sum(p_all[...], axis=0)

    def send_w(step):
        send(w_all.at[chip], w_all.at[chip], w_sem, (chip_peer(step) * 2 + core, row))

    spread(1, chips, send_w)

    settle(pb_all, chips - 1, pb_sem.at[1])
    part_b = jnp.sum(pb_all[...], axis=0)
    m_send[0] = part_b
    m_send[1, :, :i_local] = part_a
    m_all[row] = m_send[...]

    def send_m(step):
        there = lax.rem(row + step, narrow)
        send(m_send, m_all.at[row], m_sem, (me, there))

    spread(1, narrow, send_m)
    factor_b = jnp.concatenate([b_all[w % 2, w // 2] for w in range(wide)], axis=1)
    gram_b = nt(factor_b, factor_b, None)
    gram_c = nt(whole_c, whole_c)
    had_a = gram_b * gram_c
    settle(w_all, chips - 1, w_sem.at[1])
    g_all[mine] = jnp.sum(w_all[...], axis=0)

    def send_g(step):
        other, there = quad_peer(step)
        send(g_all.at[mine], g_all.at[mine], g_sem, there)

    spread(1, quad, send_g)
    fb = b_ref[...].astype(jnp.float32)
    model_a = mm(had_a, fa)
    settle(m_all, narrow - 1, m_sem.at[1])
    summed = jnp.sum(m_all[...], axis=0)
    grad_a = summed[1][:, :i_local] - model_a
    had_grad_a = mm(had_a, grad_a)

    settle(g_all, quad - 1, g_sem.at[1])
    small = g_all[...].reshape(rank, 128)
    gram_a = small[:, 2 * rank : 3 * rank]
    mttkrp_c = small[:, 3 * rank : 3 * rank + k_whole]
    had_b = gram_a * gram_c
    had_c = gram_a * gram_b
    cross_a = small[:, :rank] - mm(gram_a, had_a)
    cross_b = small[:, rank : 2 * rank] - mm(gram_b, had_b)
    cross_c = nt(whole_c, mttkrp_c) - mm(gram_c, had_c)
    grad_b = summed[0] - mm(had_b, fb)
    grad_c = mttkrp_c - mm(had_c, whole_c)
    mixed_a = cross_b * gram_c + gram_b * cross_c
    mixed_b = cross_a * gram_c + gram_a * cross_c
    mixed_c = cross_a * gram_b + gram_a * cross_b

    had_grad_b = mm(had_b, grad_b)
    had_grad_c = mm(had_c, grad_c)
    image_a = had_grad_a + mm(mixed_a, fa) + damping * grad_a
    image_b = had_grad_b + mm(mixed_b, fb) + damping * grad_b
    image_c = had_grad_c + mm(mixed_c, whole_c) + damping * grad_c
    sums = (
        total(grad_a * grad_a) + total(grad_b * grad_b),
        total(grad_a * had_grad_a) + total(grad_b * had_grad_b),
        total(image_a * image_a) + total(image_b * image_b),
        total(image_a * mm(had_a, image_a)) + total(image_b * mm(had_b, image_b)),
    )
    place = lax.broadcasted_iota(jnp.int32, (1, 128), 1)
    tile = jnp.zeros((1, 128), jnp.float32)
    for at, value in enumerate(sums):
        tile = jnp.where(place == at, value, tile)
    s_all[me] = tile

    def send_s(step):
        send(s_all.at[me], s_all.at[me], s_sem, (wide_peer(step), row))

    spread(1, wide, send_s)

    next_a = mm(cross_a, had_a) + damping * cross_a + nt(gram_a, mixed_a)
    next_b = mm(cross_b, had_b) + damping * cross_b + nt(gram_b, mixed_b)
    next_c = nt(whole_c, image_c)
    later_a = next_b * gram_c + gram_b * next_c
    later_b = next_a * gram_c + gram_a * next_c
    later_c = next_a * gram_b + gram_a * next_b
    known_gg = total(grad_c * grad_c)
    known_gh = total(grad_c * had_grad_c) + total(
        mixed_a * cross_a.T + mixed_b * cross_b.T + mixed_c * cross_c.T
    )
    known_qq = total(image_c * image_c)
    known_qh = total(image_c * mm(had_c, image_c)) + total(
        later_a * next_a.T + later_b * next_b.T + later_c * next_c.T
    )

    settle(s_all, wide - 1, s_sem.at[1])
    tile = jnp.sum(s_all[...], axis=0)
    norm_0 = tile[:, 0:1] + known_gg
    curve_0 = tile[:, 1:2] + known_gh + damping * norm_0
    image_2 = tile[:, 2:3] + known_qq
    image_3 = tile[:, 3:4] + known_qh + damping * image_2

    alpha_0 = norm_0 / curve_0
    norm_1 = norm_0 - 2.0 * alpha_0 * curve_0 + alpha_0 * alpha_0 * image_2
    beta = norm_1 / norm_0
    gain = 1.0 + beta
    curve_1 = gain * gain * curve_0 - 2.0 * gain * alpha_0 * image_2 + alpha_0 * alpha_0 * image_3
    alpha_1 = norm_1 / curve_1
    on_grad = alpha_0 + alpha_1 * gain
    on_image = -alpha_1 * alpha_0
    out_a[...] = on_grad * grad_a + on_image * image_a
    out_b[...] = on_grad * grad_b + on_image * image_b
    step_c = on_grad * grad_c + on_image * image_c
    chosen = jnp.where(
        lax.broadcasted_iota(jnp.int32, (k_whole, k_local), 0)
        == lax.broadcasted_iota(jnp.int32, (k_whole, k_local), 1) + row * k_local,
        1.0,
        0.0,
    )
    out_c[...] = mm(step_c, chosen)

    settle(c_all, narrow - 1, c_sem.at[0])
    settle(b_all.at[0], chips - 1, b_sem.at[0])
    settle(b_all.at[0], chips, relay_sem.at[0])
    settle(pb_half, chips, half_sem.at[0])
    settle(pb_all, chips - 1, pb_sem.at[0])
    settle(p_all, quad - 1, p_sem.at[0])
    settle(w_all, chips - 1, w_sem.at[0])
    settle(g_all, quad - 1, g_sem.at[0])
    settle(m_all, narrow - 1, m_sem.at[0])
    settle(s_all, wide - 1, s_sem.at[0])


def on_device(wide, narrow, tensor, factor_a, factor_b, factor_c):
    k_local, i_local, j_whole = tensor.shape
    rank, j_local = factor_b.shape
    flattened = tensor.reshape(k_local * i_local, j_whole)
    vmem = pl.BlockSpec(memory_space=pltpu.VMEM)
    anywhere = pl.BlockSpec(memory_space=pltpu.HBM)
    pair = pltpu.SemaphoreType.DMA((2,))
    f32, bf16 = jnp.float32, jnp.bfloat16
    chips, quad = wide // 2, 2 * narrow
    rows = rank // quad
    shapes = (
        jax.ShapeDtypeStruct((rank, i_local), f32),
        jax.ShapeDtypeStruct((rank, j_local), f32),
        jax.ShapeDtypeStruct((rank, k_local), f32),
    )
    step_a, step_b, step_c = pl.pallas_call(
        functools.partial(kernel, wide, narrow, k_local),
        out_shape=shapes,
        in_specs=[anywhere] * 4,
        out_specs=(vmem, vmem, vmem),
        scratch_shapes=[
            pltpu.VMEM((k_local * i_local, j_whole), bf16),
            pltpu.VMEM((rank, i_local), bf16),
            pltpu.VMEM((rank, j_local), bf16),
            pltpu.VMEM((k_local, rank), bf16),
            pltpu.VMEM((narrow, k_local, rank), bf16),
            pltpu.VMEM((2, chips, rank, j_local), bf16),
            pltpu.VMEM((2, chips, rank, j_local), f32),
            pltpu.VMEM((chips, rank, j_local), f32),
            pltpu.VMEM((chips, rank, j_local), f32),
            pltpu.VMEM((quad, rows, 128), f32),
            pltpu.VMEM((quad, rows, 128), f32),
            pltpu.VMEM((chips, rows, 128), f32),
            pltpu.VMEM((quad, rows, 128), f32),
            pltpu.VMEM((2, rank, 128), f32),
            pltpu.VMEM((narrow, 2, rank, 128), f32),
            pltpu.VMEM((wide, 1, 128), f32),
            pltpu.SemaphoreType.DMA((4,)),
            pair, pair, pair, pair, pair, pair, pair, pair, pair, pair,
        ],
        compiler_params=pltpu.CompilerParams(collective_id=0, has_side_effects=True),
    )(flattened, factor_a, factor_b, factor_c.T)
    return step_a, step_b, step_c


def solution(mesh):
    placed = (P("narrow", "wide", None), P(None, "wide"), P(None, "wide"), P(None, "narrow"))
    return jax.shard_map(
        functools.partial(on_device, mesh.shape["wide"], mesh.shape["narrow"]),
        mesh=mesh,
        in_specs=placed,
        out_specs=(P(None, "wide"), P(None, "wide"), P(None, "narrow")),
        check_vma=False,
    )
```

time: 31.6 us -> 30.1 us (0.953)
  Pallas kernels: 28 us -> 26.4 us
    pallas_call x1, Pallas kernels: 28 us -> 26.4 us  [on_device(): pl.pallas_call(functools.partial(kernel, wide, narrow, k_local), out_shap...]
    pallas_call x0 -> x1, local copies, waits for them, and re-layouts: none -> 1.36 us  [on_device(): pl.pallas_call(functools.partial(kernel, wide, narrow, k_local), out_shap...]
    unnamed x7 -> x6, local copies, waits for them, and re-layouts: 2.53 us -> 1.33 us
where the time goes in v4:
time: 30.1 us; the launch traced here: 29.7 us
  Pallas kernels  26.4 us (88%)
  local copies, waits for them, and re-layouts  2.69 us (9%)
  between operations  0.65 us (2%)
    pallas_call x1, Pallas kernels, on_device(): pl.pallas_call(functools.partial(kernel, wide, narrow, k_local), out_shap...  26.4 us
    pallas_call x1, local copies, waits for them, and re-layouts, on_device(): pl.pallas_call(functools.partial(kernel, wide, narrow, k_local), out_shap...  1.36 us
    unnamed x6, local copies, waits for them, and re-layouts  1.33 us

profile of v4, /device:TPU:0, one launch (start us, length us, event | category | flops | bytes accessed | tf_op | source)
XLA Modules:
  0.0 29.7 jit_solution(98283175219762668)
XLA Ops:
  0.6 26.4 %shard_map.67 = (f32[32,64]{1,0:T(8,128)}, f32[32,128]{1,0:T(8,128)}, f32[32,2]{1,0:T(8,128)}) custom-call(bf16[128,2048]{1,0:T(8,128)(2,1)} %bitcast.2, bf16[32,64]{1,0:T(8,128)(2,1)} %a_hbm.1, bf16[32,128]{1,0:T(8,128)(2,1)} %b_hbm.1, bf16[2,32]{1,0:T(2,128)(2,1)} %bitcast.3), custom_call_target="tpu_custom_call" | custom-call | tf_op jit(solution)/shard_map/pallas_call | solution.py:331
  27.0 0.0 copy-start.1
  27.0 1.4 %copy.7 = f32[32,2]{0,1:T(2,128)} copy(f32[32,2]{1,0:T(8,128)} %get-tuple-element.5) | data formatting | bytes 512 | tf_op jit(solution)/shard_map/pallas_call | solution.py:331
  28.4 0.0 copy-done.1
  28.4 0.0 copy-start
  28.4 0.6 %copy.10 = f32[32,64]{1,0:T(8,128)} copy(f32[32,64]{1,0:T(8,128)S(1)} %copy-done.1) | data formatting | bytes 16384
  29.0 0.1 copy-done
  29.1 0.6 %copy.11 = f32[32,128]{1,0:T(8,128)} copy(f32[32,128]{1,0:T(8,128)S(1)} %copy-done) | data formatting | bytes 32768
Async XLA Ops:
  27.0 1.4 %copy-start.1 = (f32[32,64]{1,0:T(8,128)S(1)}, f32[32,64]{1,0:T(8,128)}, u32[]{:S(2)}) copy-start(f32[32,64]{1,0:T(8,128)} %get-tuple-element.9) | copy-start | bytes 24580
  28.4 0.7 %copy-start = (f32[32,128]{1,0:T(8,128)S(1)}, f32[32,128]{1,0:T(8,128)}, u32[]{:S(2)}) copy-start(f32[32,128]{1,0:T(8,128)} %get-tuple-element.10) | copy-start | bytes 49156

commit v5 on v4

--- a/solution.py
+++ b/solution.py
@@ -41,17 +41,20 @@
 
 def kernel(
     wide, narrow, k_local, t_hbm, a_hbm, b_hbm, c_hbm, out_a, out_b, out_c,
-    t_ref, a_ref, b_ref, c_ref, c_all, b_all, pb_send, pb_half, pb_all, p_send, p_all, w_all, g_all,
+    t_ref, a_ref, b_ref, c_ref, c_all, b_all, pb_send, pb_half, pb_all, p_all, w_all,
     m_send, m_all, s_all,
-    load_sem, c_sem, b_sem, relay_sem, half_sem, pb_sem, p_sem, w_sem, g_sem, m_sem, s_sem,
+    load_sem, c_sem, b_sem, cross_sem, half_sem, pb_sem, p_sem, w_sem, m_sem, s_sem,
 ):
     me = lax.axis_index("wide")
     row = lax.axis_index("narrow")
     core = lax.rem(me, 2)
     chip = me // 2
     chips = wide // 2
-    quad = 2 * narrow
-    mine = row * 2 + core
+    low = 4 if wide % 4 == 0 else 2
+    high = wide // low
+    group = low * narrow
+    layer, side_low = me // low, lax.rem(me, low)
+    mine = row * low + side_low
     partner = (chip * 2 + 1 - core, row)
     rank, i_local = a_ref.shape
     j_local = b_ref.shape[1]
@@ -72,9 +75,12 @@
     def chip_peer(step):
         return lax.rem(chip + step, chips)
 
-    def quad_peer(step):
-        other = lax.rem(mine + step, quad)
-        return other, (chip * 2 + lax.rem(other, 2), other // 2)
+    def group_peer(step):
+        other = lax.rem(mine + step, group)
+        return layer * low + lax.rem(other, low), other // low
+
+    def layer_peer(step):
+        return lax.rem(layer + step, high) * low + side_low, row
 
     barrier = pltpu.get_barrier_semaphore()
 
@@ -83,9 +89,9 @@
 
     def greet_row(step):
         there = lax.rem(row + step, narrow)
-        for side in range(2):
+        for side in range(low):
             pl.semaphore_signal(
-                barrier, inc=1, device_id=(chip * 2 + side, there), device_id_type=MESH
+                barrier, inc=1, device_id=(layer * low + side, there), device_id_type=MESH
             )
 
     spread(1, wide, greet)
@@ -111,7 +117,7 @@
     from_k = lax.broadcasted_iota(jnp.int32, (rank, k_local * i_local), 1) // i_local
     gather_k = jnp.where(lane_k == from_k + row * k_local, 1.0, 0.0)
     gram_a_own = nt(a_ref[...], a_ref[...], None) * jnp.where(row == 0, 1.0, 0.0)
-    pl.semaphore_wait(barrier, (wide - 1) + 2 * (narrow - 1))
+    pl.semaphore_wait(barrier, (wide - 1) + low * (narrow - 1))
 
     def send(src, dst, sems, device):
         pltpu.make_async_remote_copy(
@@ -127,7 +133,12 @@
     def send_b(step):
         send(b_ref, b_all.at[core, chip], b_sem, (chip_peer(step) * 2 + core, row))
 
+    def send_b_across(step):
+        there = chip_peer(step) * 2 + 1 - core
+        send(b_ref, b_all.at[core, chip], cross_sem, (there, row))
+
     spread(1, chips, send_b)
+    spread(0, chips, send_b_across)
 
     def send_c(step):
         there = lax.rem(row + step, narrow)
@@ -150,7 +161,6 @@
         return nt(blocks, jnp.concatenate(columns, axis=1), None)
 
     settle(b_all.at[core], chips - 1, b_sem.at[1])
-    send(b_all.at[core], b_all.at[core], relay_sem, partner)
     contracted = contract(core)
     settle(pb_half, chips, half_sem.at[1])
     for at in range(chips):
@@ -162,7 +172,7 @@
 
     spread(1, chips, send_pb)
     pb_all[chip] = pb_half[chip]
-    settle(b_all.at[1 - core], chips, relay_sem.at[1])
+    settle(b_all.at[1 - core], chips, cross_sem.at[1])
     contracted = contracted + contract(1 - core)
     weighted = c_rep * contracted
     part_a = weighted[:, :i_local]
@@ -172,26 +182,23 @@
     pair_b = nt(contracted, khatri.astype(jnp.float32))
     product = a_rep * contracted
     column_c = nt(product, gather_k)
-    small = jnp.concatenate([pair_a, pair_b, gram_a_own, column_c], axis=1)
-    p_send[...] = small.reshape(p_send.shape)
+    p_all[mine] = jnp.concatenate([pair_a, pair_b, gram_a_own, column_c], axis=1)
 
     def send_p(step):
-        other, there = quad_peer(step)
-        send(p_send.at[other], p_all.at[mine], p_sem, there)
-
-    spread(1, quad, send_p)
-    p_all[mine] = p_send[mine]
+        send(p_all.at[mine], p_all.at[mine], p_sem, group_peer(step))
+
+    spread(1, group, send_p)
     settle(c_all, narrow - 1, c_sem.at[1])
     whole_c = jnp.concatenate(
         [nt(eye.astype(jnp.bfloat16), c_all[n], None) for n in range(narrow)], axis=1
     )
-    settle(p_all, quad - 1, p_sem.at[1])
-    w_all[chip] = jnp.sum(p_all[...], axis=0)
+    settle(p_all, group - 1, p_sem.at[1])
+    w_all[layer] = jnp.sum(p_all[...], axis=0)
 
     def send_w(step):
-        send(w_all.at[chip], w_all.at[chip], w_sem, (chip_peer(step) * 2 + core, row))
-
-    spread(1, chips, send_w)
+        send(w_all.at[layer], w_all.at[layer], w_sem, layer_peer(step))
+
+    spread(1, high, send_w)
 
     settle(pb_all, chips - 1, pb_sem.at[1])
     part_b = jnp.sum(pb_all[...], axis=0)
@@ -208,14 +215,6 @@
     gram_b = nt(factor_b, factor_b, None)
     gram_c = nt(whole_c, whole_c)
     had_a = gram_b * gram_c
-    settle(w_all, chips - 1, w_sem.at[1])
-    g_all[mine] = jnp.sum(w_all[...], axis=0)
-
-    def send_g(step):
-        other, there = quad_peer(step)
-        send(g_all.at[mine], g_all.at[mine], g_sem, there)
-
-    spread(1, quad, send_g)
     fb = b_ref[...].astype(jnp.float32)
     model_a = mm(had_a, fa)
     settle(m_all, narrow - 1, m_sem.at[1])
@@ -223,8 +222,8 @@
     grad_a = summed[1][:, :i_local] - model_a
     had_grad_a = mm(had_a, grad_a)
 
-    settle(g_all, quad - 1, g_sem.at[1])
-    small = g_all[...].reshape(rank, 128)
+    settle(w_all, high - 1, w_sem.at[1])
+    small = jnp.sum(w_all[...], axis=0)
     gram_a = small[:, 2 * rank : 3 * rank]
     mttkrp_c = small[:, 3 * rank : 3 * rank + k_whole]
     had_b = gram_a * gram_c
@@ -275,6 +274,14 @@
         later_a * next_a.T + later_b * next_b.T + later_c * next_c.T
     )
 
+    chosen = jnp.where(
+        lax.broadcasted_iota(jnp.int32, (k_local, k_whole), 1)
+        == lax.broadcasted_iota(jnp.int32, (k_local, k_whole), 0) + row * k_local,
+        1.0,
+        0.0,
+    )
+    own_grad_c, own_image_c = nt(chosen, grad_c), nt(chosen, image_c)
+
     settle(s_all, wide - 1, s_sem.at[1])
     tile = jnp.sum(s_all[...], axis=0)
     norm_0 = tile[:, 0:1] + known_gg
@@ -292,25 +299,28 @@
     on_image = -alpha_1 * alpha_0
     out_a[...] = on_grad * grad_a + on_image * image_a
     out_b[...] = on_grad * grad_b + on_image * image_b
-    step_c = on_grad * grad_c + on_image * image_c
-    chosen = jnp.where(
-        lax.broadcasted_iota(jnp.int32, (k_whole, k_local), 0)
-        == lax.broadcasted_iota(jnp.int32, (k_whole, k_local), 1) + row * k_local,
-        1.0,
-        0.0,
-    )
-    out_c[...] = mm(step_c, chosen)
+    out_c[...] = on_grad * own_grad_c + on_image * own_image_c
 
     settle(c_all, narrow - 1, c_sem.at[0])
     settle(b_all.at[0], chips - 1, b_sem.at[0])
-    settle(b_all.at[0], chips, relay_sem.at[0])
+    settle(b_all.at[0], chips, cross_sem.at[0])
     settle(pb_half, chips, half_sem.at[0])
     settle(pb_all, chips - 1, pb_sem.at[0])
-    settle(p_all, quad - 1, p_sem.at[0])
-    settle(w_all, chips - 1, w_sem.at[0])
-    settle(g_all, quad - 1, g_sem.at[0])
+    settle(p_all, group - 1, p_sem.at[0])
+    settle(w_all, high - 1, w_sem.at[0])
     settle(m_all, narrow - 1, m_sem.at[0])
     settle(s_all, wide - 1, s_sem.at[0])
+
+
+def write_out(in_a, in_b, in_c, out_a, out_b, out_c, sems):
+    copies = [
+        pltpu.make_async_copy(src, dst, sems.at[at])
+        for at, (src, dst) in enumerate(((in_a, out_a), (in_b, out_b), (in_c, out_c)))
+    ]
+    for copy in copies:
+        copy.start()
+    for copy in copies:
+        copy.wait()
 
 
 def on_device(wide, narrow, tensor, factor_a, factor_b, factor_c):
@@ -321,14 +331,14 @@
     anywhere = pl.BlockSpec(memory_space=pltpu.HBM)
     pair = pltpu.SemaphoreType.DMA((2,))
     f32, bf16 = jnp.float32, jnp.bfloat16
-    chips, quad = wide // 2, 2 * narrow
-    rows = rank // quad
+    chips = wide // 2
+    low = 4 if wide % 4 == 0 else 2
     shapes = (
         jax.ShapeDtypeStruct((rank, i_local), f32),
         jax.ShapeDtypeStruct((rank, j_local), f32),
-        jax.ShapeDtypeStruct((rank, k_local), f32),
-    )
-    step_a, step_b, step_c = pl.pallas_call(
+        jax.ShapeDtypeStruct((k_local, rank), f32),
+    )
+    steps = pl.pallas_call(
         functools.partial(kernel, wide, narrow, k_local),
         out_shape=shapes,
         in_specs=[anywhere] * 4,
@@ -343,19 +353,24 @@
             pltpu.VMEM((2, chips, rank, j_local), f32),
             pltpu.VMEM((chips, rank, j_local), f32),
             pltpu.VMEM((chips, rank, j_local), f32),
-            pltpu.VMEM((quad, rows, 128), f32),
-            pltpu.VMEM((quad, rows, 128), f32),
-            pltpu.VMEM((chips, rows, 128), f32),
-            pltpu.VMEM((quad, rows, 128), f32),
+            pltpu.VMEM((low * narrow, rank, 128), f32),
+            pltpu.VMEM((wide // low, rank, 128), f32),
             pltpu.VMEM((2, rank, 128), f32),
             pltpu.VMEM((narrow, 2, rank, 128), f32),
             pltpu.VMEM((wide, 1, 128), f32),
             pltpu.SemaphoreType.DMA((4,)),
-            pair, pair, pair, pair, pair, pair, pair, pair, pair, pair,
+            pair, pair, pair, pair, pair, pair, pair, pair, pair,
         ],
         compiler_params=pltpu.CompilerParams(collective_id=0, has_side_effects=True),
     )(flattened, factor_a, factor_b, factor_c.T)
-    return step_a, step_b, step_c
+    step_a, step_b, step_c = pl.pallas_call(
+        write_out,
+        out_shape=shapes,
+        in_specs=[anywhere] * 3,
+        out_specs=(anywhere,) * 3,
+        scratch_shapes=[pltpu.SemaphoreType.DMA((3,))],
+    )(*steps)
+    return step_a, step_b, step_c.T
 
 
 def solution(mesh):

time: 30.1 us -> 28 us (0.930)
  local copies, waits for them, and re-layouts: 2.69 us -> 0 us
  Pallas kernels: 26.4 us -> 27.2 us
    pallas_call x0 -> x1, Pallas kernels: none -> 2.15 us  [on_device(): pl.pallas_call(write_out, out_shape=shapes, in_specs=[anywhere] * 3, out_...]
    pallas_call x1, Pallas kernels: 26.4 us -> 25 us  [on_device(): pl.pallas_call(functools.partial(kernel, wide, narrow, k_local), out_shap...]
    pallas_call x1 -> x0, local copies, waits for them, and re-layouts: 1.36 us -> none  [on_device(): pl.pallas_call(functools.partial(kernel, wide, narrow, k_local), out_shap...]
    unnamed x6 -> x0, local copies, waits for them, and re-layouts: 1.33 us -> none
where the time goes in v5:
time: 28 us; the launch traced here: 27.8 us
  Pallas kernels  27.2 us (97%)
  between operations  0.64 us (2%)
    pallas_call x1, Pallas kernels, on_device(): pl.pallas_call(functools.partial(kernel, wide, narrow, k_local), out_shap...  25 us
    pallas_call x1, Pallas kernels, on_device(): pl.pallas_call(write_out, out_shape=shapes, in_specs=[anywhere] * 3, out_...  2.15 us

profile of v5, /device:TPU:0, one launch (start us, length us, event | category | flops | bytes accessed | tf_op | source)
XLA Modules:
  0.0 27.8 jit_solution(1357006918721530270)
XLA Ops:
  0.6 25.0 %shard_map.67 = (f32[32,64]{1,0:T(8,128)}, f32[32,128]{1,0:T(8,128)}, f32[2,32]{1,0:T(2,128)}) custom-call(bf16[128,2048]{1,0:T(8,128)(2,1)} %bitcast.3, bf16[32,64]{1,0:T(8,128)(2,1)} %a_hbm.1, bf16[32,128]{1,0:T(8,128)(2,1)} %b_hbm.1, bf16[2,32]{1,0:T(2,128)(2,1)} %bitcast.4), custom_call_target="tpu_custom_call" | custom-call | tf_op jit(solution)/shard_map/pallas_call | solution.py:341
  25.7 2.2 %shard_map.68 = (f32[32,64]{1,0:T(8,128)}, f32[32,128]{1,0:T(8,128)}, f32[2,32]{1,0:T(2,128)}) custom-call(f32[32,64]{1,0:T(8,128)} %get-tuple-element.9.in_a, f32[32,128]{1,0:T(8,128)} %get-tuple-element.10.in_b, f32[2,32]{1,0:T(2,128)} %get-tuple-element.11.in_c), custom_call_target="tpu_custom_call" | custom-call | tf_op jit(solution)/shard_map/pallas_call | solution.py:366

commit v6 on v5

--- a/solution.py
+++ b/solution.py
@@ -96,10 +96,40 @@
 
     spread(1, wide, greet)
     spread(1, narrow, greet_row)
-    for load in loads[:3]:
+    loads[0].wait()
+    b_all[core, chip] = b_ref[...]
+    pl.semaphore_wait(barrier, (wide - 1) + low * (narrow - 1))
+
+    def send(src, dst, sems, device):
+        pltpu.make_async_remote_copy(
+            src_ref=src, dst_ref=dst, send_sem=sems.at[0], recv_sem=sems.at[1],
+            device_id=device, device_id_type=MESH,
+        ).start()
+
+    def settle(buffer, count, sem):
+        if count > 0:
+            part = buffer.at[pl.ds(0, count)]
+            pltpu.make_async_copy(part, part, sem).wait()
+
+    def send_b(step):
+        send(b_ref, b_all.at[core, chip], b_sem, (chip_peer(step) * 2 + core, row))
+
+    def send_b_across(step):
+        there = chip_peer(step) * 2 + 1 - core
+        send(b_ref, b_all.at[core, chip], cross_sem, (there, row))
+
+    spread(1, chips, send_b)
+    spread(0, chips, send_b_across)
+
+    for load in loads[1:3]:
         load.wait()
-    b_all[core, chip] = b_ref[...]
     c_all[row] = c_ref[...]
+
+    def send_c(step):
+        there = lax.rem(row + step, narrow)
+        send(c_ref, c_all.at[row], c_sem, (me, there))
+
+    spread(1, narrow, send_c)
     fa = a_ref[...].astype(jnp.float32)
     eye = jnp.where(
         lax.broadcasted_iota(jnp.int32, (rank, rank), 0)
@@ -113,52 +143,34 @@
         [jnp.broadcast_to(fc[:, k : k + 1], (rank, i_local)) for k in range(k_local)], axis=1
     )
     khatri = (a_rep * c_rep).astype(jnp.bfloat16)
-    lane_k = lax.broadcasted_iota(jnp.int32, (rank, k_local * i_local), 0)
-    from_k = lax.broadcasted_iota(jnp.int32, (rank, k_local * i_local), 1) // i_local
+    slots = (128 - 3 * rank) // 2
+    lane_k = lax.broadcasted_iota(jnp.int32, (slots, k_local * i_local), 0)
+    from_k = lax.broadcasted_iota(jnp.int32, (slots, k_local * i_local), 1) // i_local
     gather_k = jnp.where(lane_k == from_k + row * k_local, 1.0, 0.0)
     gram_a_own = nt(a_ref[...], a_ref[...], None) * jnp.where(row == 0, 1.0, 0.0)
-    pl.semaphore_wait(barrier, (wide - 1) + low * (narrow - 1))
-
-    def send(src, dst, sems, device):
-        pltpu.make_async_remote_copy(
-            src_ref=src, dst_ref=dst, send_sem=sems.at[0], recv_sem=sems.at[1],
-            device_id=device, device_id_type=MESH,
-        ).start()
-
-    def settle(buffer, count, sem):
-        if count > 0:
-            part = buffer.at[pl.ds(0, count)]
-            pltpu.make_async_copy(part, part, sem).wait()
-
-    def send_b(step):
-        send(b_ref, b_all.at[core, chip], b_sem, (chip_peer(step) * 2 + core, row))
-
-    def send_b_across(step):
-        there = chip_peer(step) * 2 + 1 - core
-        send(b_ref, b_all.at[core, chip], cross_sem, (there, row))
-
-    spread(1, chips, send_b)
-    spread(0, chips, send_b_across)
-
-    def send_c(step):
-        there = lax.rem(row + step, narrow)
-        send(c_ref, c_all.at[row], c_sem, (me, there))
-
-    spread(1, narrow, send_c)
 
     loads[3].wait()
-    partial_b = jnp.dot(khatri, t_ref[...], preferred_element_type=jnp.float32)
-    for w in range(wide):
-        pb_send[w % 2, w // 2] = partial_b[:, w * j_local : (w + 1) * j_local]
+    def columns(side):
+        return jnp.concatenate(
+            [
+                t_ref[:, pl.ds(pl.multiple_of((at * 2 + side) * j_local, j_local), j_local)]
+                for at in range(chips)
+            ],
+            axis=1,
+        )
+
+    def partial_b(side):
+        part = jnp.dot(khatri, columns(side), preferred_element_type=jnp.float32)
+        for at in range(chips):
+            pb_send[side, at] = part[:, at * j_local : (at + 1) * j_local]
+
+    partial_b(1 - core)
     send(pb_send.at[1 - core], pb_half, half_sem, partner)
+    partial_b(core)
 
     def contract(side):
         blocks = jnp.concatenate([b_all[side, at] for at in range(chips)], axis=1)
-        columns = [
-            t_ref[:, pl.ds(pl.multiple_of((at * 2 + side) * j_local, j_local), j_local)]
-            for at in range(chips)
-        ]
-        return nt(blocks, jnp.concatenate(columns, axis=1), None)
+        return nt(blocks, columns(side), None)
 
     settle(b_all.at[core], chips - 1, b_sem.at[1])
     contracted = contract(core)
@@ -174,6 +186,15 @@
     pb_all[chip] = pb_half[chip]
     settle(b_all.at[1 - core], chips, cross_sem.at[1])
     contracted = contracted + contract(1 - core)
+    def packed(parts, column):
+        head = column.astype(jnp.bfloat16).astype(jnp.float32)
+        return jnp.concatenate(parts + [head, column - head], axis=1).astype(jnp.bfloat16)
+
+    def summed_small(buffer):
+        whole = jnp.sum(buffer[...].astype(jnp.float32), axis=0)
+        at = 3 * rank
+        return whole[:, :at], whole[:, at : at + slots] + whole[:, at + slots :]
+
     weighted = c_rep * contracted
     part_a = weighted[:, :i_local]
     for k in range(1, k_local):
@@ -182,7 +203,7 @@
     pair_b = nt(contracted, khatri.astype(jnp.float32))
     product = a_rep * contracted
     column_c = nt(product, gather_k)
-    p_all[mine] = jnp.concatenate([pair_a, pair_b, gram_a_own, column_c], axis=1)
+    p_all[mine] = packed([pair_a, pair_b, gram_a_own], column_c)
 
     def send_p(step):
         send(p_all.at[mine], p_all.at[mine], p_sem, group_peer(step))
@@ -192,8 +213,13 @@
     whole_c = jnp.concatenate(
         [nt(eye.astype(jnp.bfloat16), c_all[n], None) for n in range(narrow)], axis=1
     )
+    factor_b = jnp.concatenate([b_all[w % 2, w // 2] for w in range(wide)], axis=1)
+    gram_b = nt(factor_b, factor_b, None)
+    gram_c = nt(whole_c, whole_c)
+    had_a = gram_b * gram_c
     settle(p_all, group - 1, p_sem.at[1])
-    w_all[layer] = jnp.sum(p_all[...], axis=0)
+    head, column = summed_small(p_all)
+    w_all[layer] = packed([head], column)
 
     def send_w(step):
         send(w_all.at[layer], w_all.at[layer], w_sem, layer_peer(step))
@@ -211,10 +237,6 @@
         send(m_send, m_all.at[row], m_sem, (me, there))
 
     spread(1, narrow, send_m)
-    factor_b = jnp.concatenate([b_all[w % 2, w // 2] for w in range(wide)], axis=1)
-    gram_b = nt(factor_b, factor_b, None)
-    gram_c = nt(whole_c, whole_c)
-    had_a = gram_b * gram_c
     fb = b_ref[...].astype(jnp.float32)
     model_a = mm(had_a, fa)
     settle(m_all, narrow - 1, m_sem.at[1])
@@ -223,9 +245,9 @@
     had_grad_a = mm(had_a, grad_a)
 
     settle(w_all, high - 1, w_sem.at[1])
-    small = jnp.sum(w_all[...], axis=0)
+    small, column = summed_small(w_all)
     gram_a = small[:, 2 * rank : 3 * rank]
-    mttkrp_c = small[:, 3 * rank : 3 * rank + k_whole]
+    mttkrp_c = column[:, :k_whole]
     had_b = gram_a * gram_c
     had_c = gram_a * gram_b
     cross_a = small[:, :rank] - mm(gram_a, had_a)
@@ -353,8 +375,8 @@
             pltpu.VMEM((2, chips, rank, j_local), f32),
             pltpu.VMEM((chips, rank, j_local), f32),
             pltpu.VMEM((chips, rank, j_local), f32),
-            pltpu.VMEM((low * narrow, rank, 128), f32),
-            pltpu.VMEM((wide // low, rank, 128), f32),
+            pltpu.VMEM((low * narrow, rank, 128), bf16),
+            pltpu.VMEM((wide // low, rank, 128), bf16),
             pltpu.VMEM((2, rank, 128), f32),
             pltpu.VMEM((narrow, 2, rank, 128), f32),
             pltpu.VMEM((wide, 1, 128), f32),

time: 28 us -> 27.4 us (0.979)
  Pallas kernels: 27.2 us -> 26.6 us
    pallas_call x1, Pallas kernels: 25 us -> 24.4 us  [on_device(): pl.pallas_call(functools.partial(kernel, wide, narrow, k_local), out_shap...]
where the time goes in v6:
time: 27.4 us; the launch traced here: 27.2 us
  Pallas kernels  26.6 us (97%)
  between operations  0.64 us (2%)
    pallas_call x1, Pallas kernels, on_device(): pl.pallas_call(functools.partial(kernel, wide, narrow, k_local), out_shap...  24.4 us
    pallas_call x1, Pallas kernels, on_device(): pl.pallas_call(write_out, out_shape=shapes, in_specs=[anywhere] * 3, out_...  2.15 us

profile of v6, /device:TPU:0, one launch (start us, length us, event | category | flops | bytes accessed | tf_op | source)
XLA Modules:
  0.0 27.2 jit_solution(9107458825481490689)
XLA Ops:
  0.6 24.4 %shard_map.67 = (f32[32,64]{1,0:T(8,128)}, f32[32,128]{1,0:T(8,128)}, f32[2,32]{1,0:T(2,128)}) custom-call(bf16[128,2048]{1,0:T(8,128)(2,1)} %bitcast.3, bf16[32,64]{1,0:T(8,128)(2,1)} %a_hbm.1, bf16[32,128]{1,0:T(8,128)(2,1)} %b_hbm.1, bf16[2,32]{1,0:T(2,128)(2,1)} %bitcast.4), custom_call_target="tpu_custom_call" | custom-call | tf_op jit(solution)/shard_map/pallas_call | solution.py:363
  25.1 2.2 %shard_map.68 = (f32[32,64]{1,0:T(8,128)}, f32[32,128]{1,0:T(8,128)}, f32[2,32]{1,0:T(2,128)}) custom-call(f32[32,64]{1,0:T(8,128)} %get-tuple-element.9.in_a, f32[32,128]{1,0:T(8,128)} %get-tuple-element.10.in_b, f32[2,32]{1,0:T(2,128)} %get-tuple-element.11.in_c), custom_call_target="tpu_custom_call" | custom-call | tf_op jit(solution)/shard_map/pallas_call | solution.py:388

commit v7 on v6

--- a/solution.py
+++ b/solution.py
@@ -27,7 +27,7 @@
 
 
 def spread(first, last, body):
-    if last - first <= 32:
+    if last - first <= 3:
         for step in range(first, last):
             body(step)
         return
@@ -199,8 +199,8 @@
     part_a = weighted[:, :i_local]
     for k in range(1, k_local):
         part_a = part_a + weighted[:, k * i_local : (k + 1) * i_local]
-    pair_a = nt(a_rep, weighted)
-    pair_b = nt(contracted, khatri.astype(jnp.float32))
+    pair_a = nt(a_rep.astype(jnp.bfloat16), weighted.astype(jnp.bfloat16), None)
+    pair_b = nt(contracted.astype(jnp.bfloat16), khatri, None)
     product = a_rep * contracted
     column_c = nt(product, gather_k)
     p_all[mine] = packed([pair_a, pair_b, gram_a_own], column_c)

time: 27.4 us -> 27.2 us (level)
  Pallas kernels: 26.6 us -> 26.3 us
where the time goes in v7:
time: 27.2 us; the launch traced here: 27 us
  Pallas kernels  26.3 us (97%)
  between operations  0.64 us (2%)
    pallas_call x1, Pallas kernels, on_device(): pl.pallas_call(functools.partial(kernel, wide, narrow, k_local), out_shap...  24.2 us
    pallas_call x1, Pallas kernels, on_device(): pl.pallas_call(write_out, out_shape=shapes, in_specs=[anywhere] * 3, out_...  2.15 us

profile of v7, /device:TPU:0, one launch (start us, length us, event | category | flops | bytes accessed | tf_op | source)
XLA Modules:
  0.0 27.0 jit_solution(15773889681250132133)
XLA Ops:
  0.6 24.2 %shard_map.67 = (f32[32,64]{1,0:T(8,128)}, f32[32,128]{1,0:T(8,128)}, f32[2,32]{1,0:T(2,128)}) custom-call(bf16[128,2048]{1,0:T(8,128)(2,1)} %bitcast.3, bf16[32,64]{1,0:T(8,128)(2,1)} %a_hbm.1, bf16[32,128]{1,0:T(8,128)(2,1)} %b_hbm.1, bf16[2,32]{1,0:T(2,128)(2,1)} %bitcast.4), custom_call_target="tpu_custom_call" | custom-call | tf_op jit(solution)/shard_map/pallas_call | solution.py:363
  24.8 2.2 %shard_map.68 = (f32[32,64]{1,0:T(8,128)}, f32[32,128]{1,0:T(8,128)}, f32[2,32]{1,0:T(2,128)}) custom-call(f32[32,64]{1,0:T(8,128)} %get-tuple-element.9.in_a, f32[32,128]{1,0:T(8,128)} %get-tuple-element.10.in_b, f32[2,32]{1,0:T(2,128)} %get-tuple-element.11.in_c), custom_call_target="tpu_custom_call" | custom-call | tf_op jit(solution)/shard_map/pallas_call | solution.py:388

commit v8 on v7

--- a/solution.py
+++ b/solution.py
@@ -8,18 +8,34 @@
 from jax.sharding import PartitionSpec as P
 
 MESH = pl.DeviceIdType.MESH
-highest = lax.Precision.HIGHEST
 damping = 1.0
 
 
+def halves(value):
+    if value.dtype == jnp.bfloat16:
+        return (value,)
+    high = value.astype(jnp.bfloat16)
+    return high, (value - high.astype(jnp.float32)).astype(jnp.bfloat16)
+
+
+def contract_by(left, right, dims):
+    out = None
+    for at, one in enumerate(halves(left)):
+        for to, other in enumerate(halves(right)):
+            if at + to < 2:
+                term = lax.dot_general(
+                    one, other, (dims, ((), ())), preferred_element_type=jnp.float32
+                )
+                out = term if out is None else out + term
+    return out
+
+
 def mm(left, right):
-    return jnp.dot(left, right, precision=highest, preferred_element_type=jnp.float32)
-
-
-def nt(left, right, precision=highest):
-    return lax.dot_general(
-        left, right, (((1,), (1,)), ((), ())), precision=precision, preferred_element_type=jnp.float32
-    )
+    return contract_by(left, right, ((1,), (0,)))
+
+
+def nt(left, right):
+    return contract_by(left, right, ((1,), (1,)))
 
 
 def total(value):
@@ -136,8 +152,8 @@
         == lax.broadcasted_iota(jnp.int32, (rank, rank), 1),
         1.0,
         0.0,
-    )
-    fc = nt(eye.astype(jnp.bfloat16), c_ref[...], None)
+    ).astype(jnp.bfloat16)
+    fc = nt(eye, c_ref[...])
     a_rep = jnp.concatenate([fa] * k_local, axis=1)
     c_rep = jnp.concatenate(
         [jnp.broadcast_to(fc[:, k : k + 1], (rank, i_local)) for k in range(k_local)], axis=1
@@ -146,8 +162,8 @@
     slots = (128 - 3 * rank) // 2
     lane_k = lax.broadcasted_iota(jnp.int32, (slots, k_local * i_local), 0)
     from_k = lax.broadcasted_iota(jnp.int32, (slots, k_local * i_local), 1) // i_local
-    gather_k = jnp.where(lane_k == from_k + row * k_local, 1.0, 0.0)
-    gram_a_own = nt(a_ref[...], a_ref[...], None) * jnp.where(row == 0, 1.0, 0.0)
+    gather_k = jnp.where(lane_k == from_k + row * k_local, 1.0, 0.0).astype(jnp.bfloat16)
+    gram_a_own = nt(a_ref[...], a_ref[...]) * jnp.where(row == 0, 1.0, 0.0)
 
     loads[3].wait()
     def columns(side):
@@ -170,7 +186,7 @@
 
     def contract(side):
         blocks = jnp.concatenate([b_all[side, at] for at in range(chips)], axis=1)
-        return nt(blocks, columns(side), None)
+        return nt(blocks, columns(side))
 
     settle(b_all.at[core], chips - 1, b_sem.at[1])
     contracted = contract(core)
@@ -199,8 +215,8 @@
     part_a = weighted[:, :i_local]
     for k in range(1, k_local):
         part_a = part_a + weighted[:, k * i_local : (k + 1) * i_local]
-    pair_a = nt(a_rep.astype(jnp.bfloat16), weighted.astype(jnp.bfloat16), None)
-    pair_b = nt(contracted.astype(jnp.bfloat16), khatri, None)
+    pair_a = nt(a_rep.astype(jnp.bfloat16), weighted.astype(jnp.bfloat16))
+    pair_b = nt(contracted.astype(jnp.bfloat16), khatri)
     product = a_rep * contracted
     column_c = nt(product, gather_k)
     p_all[mine] = packed([pair_a, pair_b, gram_a_own], column_c)
@@ -211,10 +227,10 @@
     spread(1, group, send_p)
     settle(c_all, narrow - 1, c_sem.at[1])
     whole_c = jnp.concatenate(
-        [nt(eye.astype(jnp.bfloat16), c_all[n], None) for n in range(narrow)], axis=1
+        [nt(eye, c_all[n]).astype(jnp.bfloat16) for n in range(narrow)], axis=1
     )
     factor_b = jnp.concatenate([b_all[w % 2, w // 2] for w in range(wide)], axis=1)
-    gram_b = nt(factor_b, factor_b, None)
+    gram_b = nt(factor_b, factor_b)
     gram_c = nt(whole_c, whole_c)
     had_a = gram_b * gram_c
     settle(p_all, group - 1, p_sem.at[1])
@@ -237,7 +253,7 @@
         send(m_send, m_all.at[row], m_sem, (me, there))
 
     spread(1, narrow, send_m)
-    fb = b_ref[...].astype(jnp.float32)
+    fa, fb = a_ref[...], b_ref[...]
     model_a = mm(had_a, fa)
     settle(m_all, narrow - 1, m_sem.at[1])
     summed = jnp.sum(m_all[...], axis=0)
@@ -284,24 +300,22 @@
     next_a = mm(cross_a, had_a) + damping * cross_a + nt(gram_a, mixed_a)
     next_b = mm(cross_b, had_b) + damping * cross_b + nt(gram_b, mixed_b)
     next_c = nt(whole_c, image_c)
-    later_a = next_b * gram_c + gram_b * next_c
-    later_b = next_a * gram_c + gram_a * next_c
-    later_c = next_a * gram_b + gram_a * next_b
+    def paired(of_a, of_b, of_c):
+        return 2.0 * total(
+            of_a.T * (gram_c * of_b + gram_b * of_c) + gram_a * of_b.T * of_c
+        )
+
     known_gg = total(grad_c * grad_c)
-    known_gh = total(grad_c * had_grad_c) + total(
-        mixed_a * cross_a.T + mixed_b * cross_b.T + mixed_c * cross_c.T
-    )
+    known_gh = total(grad_c * had_grad_c) + paired(cross_a, cross_b, cross_c)
     known_qq = total(image_c * image_c)
-    known_qh = total(image_c * mm(had_c, image_c)) + total(
-        later_a * next_a.T + later_b * next_b.T + later_c * next_c.T
-    )
+    known_qh = total(image_c * mm(had_c, image_c)) + paired(next_a, next_b, next_c)
 
     chosen = jnp.where(
         lax.broadcasted_iota(jnp.int32, (k_local, k_whole), 1)
         == lax.broadcasted_iota(jnp.int32, (k_local, k_whole), 0) + row * k_local,
         1.0,
         0.0,
-    )
+    ).astype(jnp.bfloat16)
     own_grad_c, own_image_c = nt(chosen, grad_c), nt(chosen, image_c)
 
     settle(s_all, wide - 1, s_sem.at[1])
@@ -396,7 +410,7 @@
 
 
 def solution(mesh):
-    placed = (P("narrow", "wide", None), P(None, "wide"), P(None, "wide"), P(None, "narrow"))
+    placed = (P("narrow", "wide"), P(None, "wide"), P(None, "wide"), P(None, "narrow"))
     return jax.shard_map(
         functools.partial(on_device, mesh.shape["wide"], mesh.shape["narrow"]),
         mesh=mesh,

time: 27.2 us -> 27 us (level)
  no operation moved by 1% of the time
where the time goes in v8:
time: 27 us; the launch traced here: 26.8 us
  Pallas kernels  26.2 us (97%)
  between operations  0.64 us (2%)
    pallas_call x1, Pallas kernels, on_device(): pl.pallas_call(functools.partial(kernel, wide, narrow, k_local), out_shap...  24 us
    pallas_call x1, Pallas kernels, on_device(): pl.pallas_call(write_out, out_shape=shapes, in_specs=[anywhere] * 3, out_...  2.15 us

profile of v8, /device:TPU:0, one launch (start us, length us, event | category | flops | bytes accessed | tf_op | source)
XLA Modules:
  0.0 26.8 jit_solution(11322891406970594254)
XLA Ops:
  0.6 24.0 %shard_map.67 = (f32[32,64]{1,0:T(8,128)}, f32[32,128]{1,0:T(8,128)}, f32[2,32]{1,0:T(2,128)}) custom-call(bf16[128,2048]{1,0:T(8,128)(2,1)} %bitcast.3, bf16[32,64]{1,0:T(8,128)(2,1)} %a_hbm.1, bf16[32,128]{1,0:T(8,128)(2,1)} %b_hbm.1, bf16[2,32]{1,0:T(2,128)(2,1)} %bitcast.4), custom_call_target="tpu_custom_call" | custom-call | tf_op jit(solution)/shard_map/pallas_call | solution.py:377
  24.7 2.2 %shard_map.68 = (f32[32,64]{1,0:T(8,128)}, f32[32,128]{1,0:T(8,128)}, f32[2,32]{1,0:T(2,128)}) custom-call(f32[32,64]{1,0:T(8,128)} %get-tuple-element.9.in_a, f32[32,128]{1,0:T(8,128)} %get-tuple-element.10.in_b, f32[2,32]{1,0:T(2,128)} %get-tuple-element.11.in_c), custom_call_target="tpu_custom_call" | custom-call | tf_op jit(solution)/shard_map/pallas_call | solution.py:402

commit v9 on v8

--- a/solution.py
+++ b/solution.py
@@ -56,10 +56,11 @@
 
 
 def kernel(
-    wide, narrow, k_local, t_hbm, a_hbm, b_hbm, c_hbm, out_a, out_b, out_c,
+    wide, narrow, k_local, t_hbm, a_hbm, b_hbm, c_hbm, a_out, b_out, c_out,
+    out_a, out_b, out_c,
     t_ref, a_ref, b_ref, c_ref, c_all, b_all, pb_send, pb_half, pb_all, p_all, w_all,
     m_send, m_all, s_all,
-    load_sem, c_sem, b_sem, cross_sem, half_sem, pb_sem, p_sem, w_sem, m_sem, s_sem,
+    load_sem, out_sem, c_sem, b_sem, cross_sem, half_sem, pb_sem, p_sem, w_sem, m_sem, s_sem,
 ):
     me = lax.axis_index("wide")
     row = lax.axis_index("narrow")
@@ -336,6 +337,12 @@
     out_a[...] = on_grad * grad_a + on_image * image_a
     out_b[...] = on_grad * grad_b + on_image * image_b
     out_c[...] = on_grad * own_grad_c + on_image * own_image_c
+    stores = [
+        pltpu.make_async_copy(src, dst, out_sem.at[at])
+        for at, (src, dst) in enumerate(((out_a, a_out), (out_b, b_out), (out_c, c_out)))
+    ]
+    for store in stores:
+        store.start()
 
     settle(c_all, narrow - 1, c_sem.at[0])
     settle(b_all.at[0], chips - 1, b_sem.at[0])
@@ -346,24 +353,26 @@
     settle(w_all, high - 1, w_sem.at[0])
     settle(m_all, narrow - 1, m_sem.at[0])
     settle(s_all, wide - 1, s_sem.at[0])
-
-
-def write_out(in_a, in_b, in_c, out_a, out_b, out_c, sems):
-    copies = [
-        pltpu.make_async_copy(src, dst, sems.at[at])
-        for at, (src, dst) in enumerate(((in_a, out_a), (in_b, out_b), (in_c, out_c)))
-    ]
-    for copy in copies:
-        copy.start()
-    for copy in copies:
-        copy.wait()
+    for store in stores:
+        store.wait()
+
+
+def write_out(in_a, in_b, in_c, out_a, out_b, out_c, held_a, held_b, held_c, sems):
+    held = (held_a, held_b, held_c)
+    for at, pairs in enumerate((zip((in_a, in_b, in_c), held), zip(held, (out_a, out_b, out_c)))):
+        copies = [
+            pltpu.make_async_copy(src, dst, sems.at[at, to]) for to, (src, dst) in enumerate(pairs)
+        ]
+        for copy in copies:
+            copy.start()
+        for copy in copies:
+            copy.wait()
 
 
 def on_device(wide, narrow, tensor, factor_a, factor_b, factor_c):
     k_local, i_local, j_whole = tensor.shape
     rank, j_local = factor_b.shape
     flattened = tensor.reshape(k_local * i_local, j_whole)
-    vmem = pl.BlockSpec(memory_space=pltpu.VMEM)
     anywhere = pl.BlockSpec(memory_space=pltpu.HBM)
     pair = pltpu.SemaphoreType.DMA((2,))
     f32, bf16 = jnp.float32, jnp.bfloat16
@@ -374,12 +383,14 @@
         jax.ShapeDtypeStruct((rank, j_local), f32),
         jax.ShapeDtypeStruct((k_local, rank), f32),
     )
+    held = [pltpu.VMEM(one.shape, f32) for one in shapes]
     steps = pl.pallas_call(
         functools.partial(kernel, wide, narrow, k_local),
         out_shape=shapes,
         in_specs=[anywhere] * 4,
-        out_specs=(vmem, vmem, vmem),
+        out_specs=(anywhere,) * 3,
         scratch_shapes=[
+            *held,
             pltpu.VMEM((k_local * i_local, j_whole), bf16),
             pltpu.VMEM((rank, i_local), bf16),
             pltpu.VMEM((rank, j_local), bf16),
@@ -395,6 +406,7 @@
             pltpu.VMEM((narrow, 2, rank, 128), f32),
             pltpu.VMEM((wide, 1, 128), f32),
             pltpu.SemaphoreType.DMA((4,)),
+            pltpu.SemaphoreType.DMA((3,)),
             pair, pair, pair, pair, pair, pair, pair, pair, pair,
         ],
         compiler_params=pltpu.CompilerParams(collective_id=0, has_side_effects=True),
@@ -404,7 +416,7 @@
         out_shape=shapes,
         in_specs=[anywhere] * 3,
         out_specs=(anywhere,) * 3,
-        scratch_shapes=[pltpu.SemaphoreType.DMA((3,))],
+        scratch_shapes=[*held, pltpu.SemaphoreType.DMA((2, 3))],
     )(*steps)
     return step_a, step_b, step_c.T
 

time: 27 us -> 26.4 us (0.978)
  Pallas kernels: 26.2 us -> 25.4 us
    pallas_call x1, Pallas kernels: 2.15 us -> 1.4 us  [on_device(): pl.pallas_call(write_out, out_shape=shapes, in_specs=[anywhere] * 3, out_...]
where the time goes in v9:
time: 26.4 us; the launch traced here: 26.1 us
  Pallas kernels  25.4 us (96%)
  between operations  0.64 us (2%)
    pallas_call x1, Pallas kernels, on_device(): pl.pallas_call(functools.partial(kernel, wide, narrow, k_local), out_shap...  24 us
    pallas_call x1, Pallas kernels, on_device(): pl.pallas_call(write_out, out_shape=shapes, in_specs=[anywhere] * 3, out_...  1.4 us

profile of v9, /device:TPU:0, one launch (start us, length us, event | category | flops | bytes accessed | tf_op | source)
XLA Modules:
  0.0 26.1 jit_solution(5418639612733070995)
XLA Ops:
  0.6 24.0 %shard_map.67 = (f32[32,64]{1,0:T(8,128)}, f32[32,128]{1,0:T(8,128)}, f32[2,32]{1,0:T(2,128)}) custom-call(bf16[128,2048]{1,0:T(8,128)(2,1)} %bitcast.3, bf16[32,64]{1,0:T(8,128)(2,1)} %a_hbm.1, bf16[32,128]{1,0:T(8,128)(2,1)} %b_hbm.1, bf16[2,32]{1,0:T(2,128)(2,1)} %bitcast.4), custom_call_target="tpu_custom_call" | custom-call | tf_op jit(solution)/shard_map/pallas_call | solution.py:387
  24.7 1.4 %shard_map.68 = (f32[32,64]{1,0:T(8,128)}, f32[32,128]{1,0:T(8,128)}, f32[2,32]{1,0:T(2,128)}) custom-call(f32[32,64]{1,0:T(8,128)} %get-tuple-element.9.in_a, f32[32,128]{1,0:T(8,128)} %get-tuple-element.10.in_b, f32[2,32]{1,0:T(2,128)} %get-tuple-element.11.in_c), custom_call_target="tpu_custom_call" | custom-call | tf_op jit(solution)/shard_map/pallas_call | solution.py:414
